TPU v7x, 128 devices: a whole 4x4x4 slice. The times are simulated.
128 devices in a mesh: band: 16 (over x, z), mesh: 8 (over y, core).
Axes of the slice: x: 4, y: 4, z: 4, core: 2. Of those that a mesh axis runs over, the one named last changes fastest.
Arguments:
- grid_latent: bfloat16 [131072, 512], P(('band', 'mesh')), may hold values from -6 to 6
- mesh_latent: bfloat16 [8192, 512], P(('band', 'mesh')), may hold values from -6 to 6
- w_src_enc: bfloat16 [512, 512], replicated, may hold values from -0.25 to 0.25
- w_dst_enc: bfloat16 [512, 512], replicated, may hold values from -0.25 to 0.25
- w_out_enc: bfloat16 [512, 512], replicated, may hold values from -0.25 to 0.25
- w_src_dec: bfloat16 [512, 512], replicated, may hold values from -0.25 to 0.25
- w_dst_dec: bfloat16 [512, 512], replicated, may hold values from -0.25 to 0.25
- w_out_dec: bfloat16 [512, 512], replicated, may hold values from -0.25 to 0.25
- grid_cot: bfloat16 [131072, 512], P(('band', 'mesh')), may hold values from -6 to 6
- enc_send: int32 [128, 3, 3, 128], P(('band', 'mesh')), may hold values from 0 to 1023
- enc_slot: int32 [8192, 32], P(('band', 'mesh')), may hold values from 0 to 1151, as said below
- enc_count: int32 [8192], P(('band', 'mesh')), may hold values from 1 to 32
- dec_send: int32 [128, 3, 3, 128], P(('band', 'mesh')), may hold values from 0 to 63
- dec_slot: int32 [131072, 3], P(('band', 'mesh')), may hold values from 0 to 1151, as said below
- dec_count: int32 [131072], P(('band', 'mesh')), may hold values from 1 to 3
Outputs:
- grid_grad: float32 [131072, 512], P(('band', 'mesh'))
- mesh_grad: float32 [8192, 512], P(('band', 'mesh'))
- grad_src_enc: float32 [512, 512], replicated
- grad_dst_enc: float32 [512, 512], replicated
- grad_out_enc: float32 [512, 512], replicated
- grad_src_dec: float32 [512, 512], replicated
- grad_dst_dec: float32 [512, 512], replicated
- grad_out_dec: float32 [512, 512], replicated
Inputs may be any that keep to these rules, and one draw needn't show every extreme that they name: enc_send[p, a, e, c] is a row among device p's 1024 grid nodes; rows may repeat. `enc_slot`: a receive row s = (a * 3 + e) * 128 + c of the mesh node's device whose sender's band b + a - 1 exists (0 to 16 - 1). dec_send[p, a, e, c] is a row among device p's 64 mesh nodes; rows may repeat. `dec_slot`: a receive row s = (a * 3 + e) * 128 + c of the grid node's device whose sender's band b + a - 1 exists (0 to 16 - 1).
All inputs are finite; a program needn't handle non-finite values.
Results may differ from a plain program's by a relative error of at most 0.02.
Values may be sent and summed in bfloat16 or wider, within the bound.
No kernel may reach another device: no remote copies, remote signals or barrier semaphores. Data moves between devices by JAX's collectives and lax.ppermute only.
A program may use at most 128 MiB of HBM per device.

v0:
```python
import jax
import jax.numpy as jnp
from jax import lax
from jax.sharding import PartitionSpec as P


def padded(x, sides, width, wrap):
    for axis, dim in sides:
        count, length = (lax.axis_size(axis), x.shape[dim])
        up = [(i, (i + 1) % count) for i in range(count if wrap else count - 1)]
        down = [(j, i) for i, j in up]
        last = lax.slice_in_dim(x, length - width, length, axis=dim)
        initial = lax.slice_in_dim(x, 0, width, axis=dim)
        before = lax.ppermute(last, axis, up)
        after = lax.ppermute(initial, axis, down)
        x = jnp.concatenate([before, x, after], axis=dim)
    return x


def silu_slope(values):
    squashed = jax.nn.sigmoid(values)
    return squashed * (1.0 + values * (1.0 - squashed))


def edge_weight(counts, fanout):
    places = jnp.arange(fanout, dtype=jnp.int32)[None, :]
    live = (places < counts[:, None]).astype(jnp.float32)
    return live / counts[:, None].astype(jnp.float32)


def forward_side(received, latent, slots, counts, w_source, w_target):
    source_proj = jnp.dot(received, w_source, preferred_element_type=jnp.float32)
    target_proj = jnp.dot(latent, w_target, preferred_element_type=jnp.float32)
    before = source_proj[slots] + target_proj[:, None, :]
    weights = edge_weight(counts, slots.shape[1])
    mean_msg = jnp.sum(jax.nn.silu(before) * weights[:, :, None], axis=1).astype(jnp.bfloat16)
    return (before, weights, mean_msg)


def backward_side(
    received, latent, slots, before, weights, upstream, w_source, w_target, slot_count
):
    width = before.shape[2]
    d_before = (upstream[:, None, :] * weights[:, :, None] * silu_slope(before)).astype(
        jnp.bfloat16
    )
    target_sum = jnp.sum(d_before, axis=1, dtype=jnp.float32).astype(jnp.bfloat16)
    target_grad = jnp.dot(latent.T, target_sum, preferred_element_type=jnp.float32)
    direct = jnp.dot(target_sum, w_target.T, preferred_element_type=jnp.float32)
    slot_sum = jax.ops.segment_sum(
        d_before.reshape(-1, width).astype(jnp.float32), slots.reshape(-1), num_segments=slot_count
    ).astype(jnp.bfloat16)
    source_grad = jnp.dot(received.T, slot_sum, preferred_element_type=jnp.float32)
    sent_back = jnp.dot(slot_sum, w_source.T, preferred_element_type=jnp.float32).astype(
        jnp.bfloat16
    )
    return (target_grad, direct, source_grad, sent_back)


def neighbours(rows, capacity):
    blocks = rows.reshape(3, 3, capacity, rows.shape[-1])
    across = padded(blocks, (("mesh", 1),), 1, True)[:, ::2]
    arrived = padded(across, (("band", 0),), 1, False)[::2]
    return arrived.reshape(rows.shape)


def body(
    grid_latent,
    mesh_latent,
    w_src_enc,
    w_dst_enc,
    w_out_enc,
    w_src_dec,
    w_dst_dec,
    w_out_dec,
    grid_cot,
    enc_send,
    enc_slot,
    enc_count,
    dec_send,
    dec_slot,
    dec_count,
):
    grid_rows = grid_latent.shape[0]
    mesh_rows = mesh_latent.shape[0]
    enc_cap = enc_send.shape[3]
    dec_cap = dec_send.shape[3]
    enc_index = enc_send.reshape(-1)
    dec_index = dec_send.reshape(-1)
    received_grid = neighbours(grid_latent[enc_index], enc_cap)
    enc_before, enc_weights, enc_mean = forward_side(
        received_grid, mesh_latent, enc_slot, enc_count, w_src_enc, w_dst_enc
    )
    mesh_new = (
        mesh_latent.astype(jnp.float32)
        + jnp.dot(enc_mean, w_out_enc, preferred_element_type=jnp.float32)
    ).astype(jnp.bfloat16)
    received_mesh = neighbours(mesh_new[dec_index], dec_cap)
    dec_before, dec_weights, dec_mean = forward_side(
        received_mesh, grid_latent, dec_slot, dec_count, w_src_dec, w_dst_dec
    )
    dec_upstream = jnp.dot(grid_cot, w_out_dec.T, preferred_element_type=jnp.float32)
    output_grad_dec = jnp.dot(dec_mean.T, grid_cot, preferred_element_type=jnp.float32)
    target_grad_dec, direct_grid, source_grad_dec, mesh_sent = backward_side(
        received_mesh,
        grid_latent,
        dec_slot,
        dec_before,
        dec_weights,
        dec_upstream,
        w_src_dec,
        w_dst_dec,
        received_mesh.shape[0],
    )
    mesh_home = neighbours(mesh_sent, dec_cap)
    mesh_dnew = jax.ops.segment_sum(
        mesh_home.astype(jnp.float32), dec_index, num_segments=mesh_rows
    )
    dnew_round = mesh_dnew.astype(jnp.bfloat16)
    enc_upstream = jnp.dot(dnew_round, w_out_enc.T, preferred_element_type=jnp.float32)
    output_grad_enc = jnp.dot(enc_mean.T, dnew_round, preferred_element_type=jnp.float32)
    target_grad_enc, direct_mesh, source_grad_enc, grid_sent = backward_side(
        received_grid,
        mesh_latent,
        enc_slot,
        enc_before,
        enc_weights,
        enc_upstream,
        w_src_enc,
        w_dst_enc,
        received_grid.shape[0],
    )
    grid_home = neighbours(grid_sent, enc_cap)
    grid_grad = (
        grid_cot.astype(jnp.float32)
        + direct_grid
        + jax.ops.segment_sum(grid_home.astype(jnp.float32), enc_index, num_segments=grid_rows)
    )
    mesh_grad = mesh_dnew + direct_mesh
    summed = lax.psum(
        (
            source_grad_enc,
            target_grad_enc,
            output_grad_enc,
            source_grad_dec,
            target_grad_dec,
            output_grad_dec,
        ),
        ("band", "mesh"),
    )
    return (grid_grad, mesh_grad, summed[0], summed[1], summed[2], summed[3], summed[4], summed[5])


def solution(mesh):
    return jax.shard_map(
        body,
        mesh=mesh,
        in_specs=(
            P(("band", "mesh"), None),
            P(("band", "mesh"), None),
            P(),
            P(),
            P(),
            P(),
            P(),
            P(),
            P(("band", "mesh"), None),
            P(("band", "mesh"), None, None, None),
            P(("band", "mesh"), None),
            P(("band", "mesh")),
            P(("band", "mesh"), None, None, None),
            P(("band", "mesh"), None),
            P(("band", "mesh")),
        ),
        out_specs=(
            P(("band", "mesh"), None),
            P(("band", "mesh"), None),
            P(),
            P(),
            P(),
            P(),
            P(),
            P(),
        ),
        check_vma=False,
    )
```

profile of v0, /device:TPU:1, one launch (start us, length us, event | category | flops | bytes accessed | tf_op | source)
XLA Modules:
  0.0 434.5 jit_solution(15368353046406551424)
XLA Ops:
  8.4 4.2 gather_fusion
  30.0 6.4 %collective-permute-done.2 = bf16[1,3,128,512]{3,2,1,0:T(8,128)(2,1)S(1)} collective-permute-done((bf16[1,3,128,512]{3,2,1,0:T(8,128)(2,1)S(1)}, bf16[1,3,128,512]{3,2,1,0:T(8,128)(2,1)S(1)}, u32[]{:S(2)}, u32[]{:S(2)}) %collective-permute-start.2) | collective-permute-done | bytes 393248 | tf_op jit(solution)/shard_map/ppermute | solution.py:14
  42.6 8.9 %gather_fusion.1 = f32[2048,512]{1,0:T(8,128)} fusion(f32[1152,512]{1,0:T(8,128)S(1)} %fusion.46, s32[2048]{0:T(1024)S(1)} %broadcast_clamp_fusion.1), kind=kCustom, calls=%fused_computation.1 | custom fusion | bytes 8396800 | tf_op jit(solution)/shard_map/gather | solution.py:34
  51.5 4.6 %multiply_reduce_fusion.1 = (bf16[64,512]{1,0:T(8,128)(2,1)S(1)}, f32[64,32,512]{2,1,0:T(8,128)}) fusion(f32[64,32]{1,0:T(8,128)S(1)} %convert_divide_fusion.1, f32[64,512]{1,0:T(8,128)} %fusion.47, f32[2048,512]{1,0:T(8,128)} %gather_fusion.1), kind=kLoop, calls=%fused_computation.28 | loop fusion | flops 7307264 | bytes 8593408 | tf_op jit(solution)/shard_map/reduce_sum | solution.py:36
  57.0 4.2 gather_fusion.2
  73.1 4.4 %collective-permute-start.6 = (bf16[1,3,128,512]{3,2,1,0:T(8,128)(2,1)}, bf16[1,3,128,512]{3,2,1,0:T(8,128)(2,1)}, u32[]{:S(2)}, u32[]{:S(2)}) collective-permute-start(bf16[1,3,128,512]{3,2,1,0:T(8,128)(2,1)} %get-tuple-element.42), channel_id=1, source_target_pairs={{0,8},{8,16},{16,24},{24,32},{32,40},{40,48},{48,56},{56,64},{64,7... | collective-permute-start | bytes 1179656 | tf_op jit(solution)/shard_map/ppermute | solution.py:14
  83.6 4.7 %mul.96 = f32[1024,3,512]{2,1,0:T(4,128)} broadcast(f32[1024,512]{1,0:T(8,128)S(1)} %fusion.45), dimensions={0,2} | broadcast | bytes 8388608 | tf_op jit(solution)/shard_map/mul | solution.py:44
  88.3 10.8 %mul.105 = f32[3072,512]{1,0:T(8,128)} reshape(f32[1024,3,512]{2,1,0:T(4,128)} %mul.96) | data formatting | bytes 12582912 | tf_op jit(solution)/shard_map/mul | solution.py:44
  104.5 12.8 %gather_fusion.3 = f32[3072,512]{1,0:T(8,128)} fusion(f32[1152,512]{1,0:T(8,128)S(1)} %fusion.48, s32[3072]{0:T(1024)S(1)} %broadcast_clamp_fusion), kind=kCustom, calls=%fused_computation.3 | custom fusion | bytes 12595200 | tf_op jit(solution)/shard_map/gather | solution.py:34
  117.3 10.7 %reshape.245 = f32[1024,3,512]{2,1,0:T(4,128)} reshape(f32[3072,512]{1,0:T(8,128)} %gather_fusion.3) | data formatting | bytes 12582912 | tf_op jit(solution)/shard_map/gather | solution.py:34
  128.0 13.1 %multiply_reduce_fusion = (bf16[1024,512]{1,0:T(8,128)(2,1)}, f32[1024,3,512]{2,1,0:T(4,128)}) fusion(f32[1024,3]{1,0:T(8,128)} %convert_divide_fusion, f32[1024,3,512]{2,1,0:T(4,128)} %reshape.245, f32[1024,512]{1,0:T(8,128)S(1)} %copy-done.7), kind=kLoop, calls=%fused_computation.8 | loop fusion | flops 10485760 | bytes 15740928 | tf_op jit(solution)/shard_map/reduce_sum | solution.py:36
  141.1 10.8 %add.138 = f32[3072,512]{1,0:T(8,128)} reshape(f32[1024,3,512]{2,1,0:T(4,128)} %get-tuple-element.31) | data formatting | bytes 12582912 | tf_op jit(solution)/shard_map/add | solution.py:34
  151.9 23.4 %scatter_custom_fusion = f32[1152,512]{1,0:T(8,128)S(1)} fusion(s32[3072]{0:T(1024)S(1)} %reshape.254, f32[3072,512]{1,0:T(8,128)} %add.138, f32[3072,512]{1,0:T(8,128)} %mul.105, f32[]{:T(128)} %constant.7.clone.1, f32[3072]{0:T(1024)S(1)} %div.54, f32[]{:T(128)} %constant.11.clone.1), kind=kCustom, calls=%fused_computation.11 | custom fusion | flops 18874368 | bytes 14954504 | tf_op jit(solution)/shard_map/scatter-add | solution.py:50
  178.6 12.0 %fusion.11 = bf16[1024,512]{1,0:T(8,128)(2,1)S(1)} fusion(f32[1024,3,512]{2,1,0:T(4,128)} %get-tuple-element.31, f32[1024,3]{1,0:T(8,128)S(1)} %copy-done.10, f32[1024,512]{1,0:T(8,128)S(1)} %copy-done.3), kind=kLoop, calls=%fused_computation.30 | loop fusion | flops 16777216 | bytes 9449472 | tf_op jit(solution)/shard_map/reduce_sum | solution.py:47
  192.8 4.3 collective-permute-start.10
  206.9 10.7 %scatter_custom_fusion.1 = f32[64,512]{1,0:T(8,128)S(1)} fusion(s32[1152]{0:T(1024)} %reshape.262, bf16[1152,512]{1,0:T(8,128)(2,1)S(1)} %bitcast.82, f32[]{:T(128)} %constant.11.clone.1), kind=kCustom, calls=%fused_computation.35 | custom fusion | flops 1179648 | bytes 1311232 | tf_op jit(solution)/shard_map/scatter-add | solution.py:116
  219.2 4.3 fusion.16
  226.3 13.9 %scatter_custom_fusion.2 = f32[1152,512]{1,0:T(8,128)S(1)} fusion(s32[2048]{0:T(1024)S(1)} %reshape.270, bf16[2048,512]{1,0:T(8,128)(2,1)} %fusion.8, f32[]{:T(128)} %constant.11.clone.1), kind=kCustom, calls=%fused_computation.25 | custom fusion | flops 2097152 | bytes 4456452 | tf_op jit(solution)/shard_map/scatter-add | solution.py:50
  247.6 4.6 %collective-permute-start.12 = (bf16[3,1,128,512]{3,2,1,0:T(8,128)(2,1)S(1)}, bf16[3,1,128,512]{3,2,1,0:T(8,128)(2,1)S(1)}, u32[]{:S(2)}, u32[]{:S(2)}) collective-permute-start(bf16[3,1,128,512]{3,2,1,0:T(8,128)(2,1)S(1)} %get-tuple-element.36), channel_id=1, source_target_pairs={{0,1},{1,2},{2,3},{3,4},{4,5},{5,6},{6,7},{7,0},{8,9},{9,10},{10,1... | collective-permute-start | bytes 1179656 | tf_op jit(solution)/shard_map/ppermute | solution.py:14
  252.2 4.7 %collective-permute-done.12 = bf16[3,1,128,512]{3,2,1,0:T(8,128)(2,1)S(1)} collective-permute-done((bf16[3,1,128,512]{3,2,1,0:T(8,128)(2,1)S(1)}, bf16[3,1,128,512]{3,2,1,0:T(8,128)(2,1)S(1)}, u32[]{:S(2)}, u32[]{:S(2)}) %collective-permute-start.12) | collective-permute-done | bytes 393248 | tf_op jit(solution)/shard_map/ppermute | solution.py:14
  269.1 7.0 %collective-permute-done.14 = bf16[1,3,128,512]{3,2,1,0:T(8,128)(2,1)S(1)} collective-permute-done((bf16[1,3,128,512]{3,2,1,0:T(8,128)(2,1)S(1)}, bf16[1,3,128,512]{3,2,1,0:T(8,128)(2,1)S(1)}, u32[]{:S(2)}, u32[]{:S(2)}) %collective-permute-start.14) | collective-permute-done | bytes 393248 | tf_op jit(solution)/shard_map/ppermute | solution.py:14
  276.1 4.5 %collective-permute-done.15 = bf16[1,3,128,512]{3,2,1,0:T(8,128)(2,1)S(1)} collective-permute-done((bf16[1,3,128,512]{3,2,1,0:T(8,128)(2,1)S(1)}, bf16[1,3,128,512]{3,2,1,0:T(8,128)(2,1)S(1)}, u32[]{:S(2)}, u32[]{:S(2)}) %collective-permute-start.15) | collective-permute-done | bytes 393248 | tf_op jit(solution)/shard_map/ppermute | solution.py:15
  280.9 13.0 %scatter_custom_fusion.3 = f32[1024,512]{1,0:T(8,128)} fusion(f32[1024,512]{1,0:T(8,128)} %convert_add_fusion, s32[1152]{0:T(1024)S(1)} %reshape.278, bf16[1152,512]{1,0:T(8,128)(2,1)S(1)} %bitcast.81), kind=kCustom, calls=%fused_computation.33 | custom fusion | flops 1179648 | bytes 3276800 | tf_op jit(solution)/shard_map/scatter-add | solution.py:137
  293.9 124.2 %all-reduce.3.cloned.1.call-done = (f32[512,512]{1,0:T(8,128)}, f32[512,512]{0,1:T(8,128)}, f32[512,512]{1,0:T(8,128)}, f32[512,512]{1,0:T(8,128)}, f32[512,512]{0,1:T(8,128)}, /*index=5*/f32[512,512]{1,0:T(8,128)}) async-done(((f32[512,512]{1,0:T(8,128)}, f32[512,512]{0,1:T(8,128)}, f32[512,512]{1,0:T(8,128)}, f32[512,512]{1,0:T(8,128)}, f32[512,512]{0,1:T(8,128)}, /*index=5*/f32[512,512]{1,0:T(8,128)}), ...) | async-done | bytes 6291472 | tf_op jit(solution)/shard_map/psum | solution.py:140
  (191 shorter events, 97.2 us)
Async XLA Ops:
  7.2 410.9 %all-reduce.3.cloned.1.call-start = ((), (), s32[]{:S(2)}) async-start(), calls=%async_computation | async-start | bytes 12582912 | tf_op jit(solution)/shard_map/psum | solution.py:140
  12.7 7.4 %collective-permute-start = (bf16[3,1,128,512]{3,2,1,0:T(8,128)(2,1)S(1)}, bf16[3,1,128,512]{3,2,1,0:T(8,128)(2,1)S(1)}, u32[]{:S(2)}, u32[]{:S(2)}) collective-permute-start(bf16[3,1,128,512]{3,2,1,0:T(8,128)(2,1)S(1)} %get-tuple-element.48), channel_id=1, source_target_pairs={{0,1},{1,2},{2,3},{3,4},{4,5},{5,6},{6,7},{7,0},{8,9},{9,10},{10,1... | collective-permute-start | bytes 1179656 | tf_op jit(solution)/shard_map/ppermute | solution.py:14
  15.4 7.3 %collective-permute-start.1 = (bf16[3,1,128,512]{3,2,1,0:T(8,128)(2,1)S(1)}, bf16[3,1,128,512]{3,2,1,0:T(8,128)(2,1)}, u32[]{:S(2)}, u32[]{:S(2)}) collective-permute-start(bf16[3,1,128,512]{3,2,1,0:T(8,128)(2,1)S(1)} %get-tuple-element.49), channel_id=1, source_target_pairs={{1,0},{2,1},{3,2},{4,3},{5,4},{6,5},{7,6},{0,7},{9,8},{10,9},{11,1... | collective-permute-start | bytes 1179656 | tf_op jit(solution)/shard_map/ppermute | solution.py:15
  15.7 63.3 %copy-start.37 = (f32[64,32]{1,0:T(8,128)}, f32[64,32]{1,0:T(8,128)S(1)}, u32[]{:S(2)}) copy-start(f32[64,32]{1,0:T(8,128)S(1)} %convert_divide_fusion.1) | copy-start | bytes 24580
  24.2 12.2 %collective-permute-start.2 = (bf16[1,3,128,512]{3,2,1,0:T(8,128)(2,1)S(1)}, bf16[1,3,128,512]{3,2,1,0:T(8,128)(2,1)S(1)}, u32[]{:S(2)}, u32[]{:S(2)}) collective-permute-start(bf16[1,3,128,512]{3,2,1,0:T(8,128)(2,1)S(1)} %get-tuple-element.46), channel_id=1, source_target_pairs={{0,8},{8,16},{16,24},{24,32},{32,40},{40,48},{48,56},{56,64},{64,7... | collective-permute-start | bytes 1179656 | tf_op jit(solution)/shard_map/ppermute | solution.py:14
  27.8 12.8 %collective-permute-start.3 = (bf16[1,3,128,512]{3,2,1,0:T(8,128)(2,1)S(1)}, bf16[1,3,128,512]{3,2,1,0:T(8,128)(2,1)S(1)}, u32[]{:S(2)}, u32[]{:S(2)}) collective-permute-start(bf16[1,3,128,512]{3,2,1,0:T(8,128)(2,1)S(1)} %get-tuple-element.47), channel_id=1, source_target_pairs={{8,0},{16,8},{24,16},{32,24},{40,32},{48,40},{56,48},{64,56},{72,6... | collective-permute-start | bytes 1179656 | tf_op jit(solution)/shard_map/ppermute | solution.py:15
  30.0 11.9 %copy-start.25 = (bf16[512,512]{1,0:T(8,128)(2,1)S(1)}, bf16[512,512]{1,0:T(8,128)(2,1)}, u32[]{:S(2)}) copy-start(bf16[512,512]{1,0:T(8,128)(2,1)} %param.17) | copy-start | bytes 1572868
  62.2 5.7 %collective-permute-start.4 = (bf16[3,1,128,512]{3,2,1,0:T(8,128)(2,1)}, bf16[3,1,128,512]{3,2,1,0:T(8,128)(2,1)}, u32[]{:S(2)}, u32[]{:S(2)}) collective-permute-start(bf16[3,1,128,512]{3,2,1,0:T(8,128)(2,1)} %get-tuple-element.44), channel_id=1, source_target_pairs={{0,1},{1,2},{2,3},{3,4},{4,5},{5,6},{6,7},{7,0},{8,9},{9,10},{10,1... | collective-permute-start | bytes 1179656 | tf_op jit(solution)/shard_map/ppermute | solution.py:14
  62.9 7.8 %collective-permute-start.5 = (bf16[3,1,128,512]{3,2,1,0:T(8,128)(2,1)}, bf16[3,1,128,512]{3,2,1,0:T(8,128)(2,1)}, u32[]{:S(2)}, u32[]{:S(2)}) collective-permute-start(bf16[3,1,128,512]{3,2,1,0:T(8,128)(2,1)} %get-tuple-element.45), channel_id=1, source_target_pairs={{1,0},{2,1},{3,2},{4,3},{5,4},{6,5},{7,6},{0,7},{9,8},{10,9},{11,1... | collective-permute-start | bytes 1179656 | tf_op jit(solution)/shard_map/ppermute | solution.py:15
  65.8 17.8 %copy-start.2 = (f32[1024,512]{1,0:T(8,128)}, f32[1024,512]{1,0:T(8,128)S(1)}, u32[]{:S(2)}) copy-start(f32[1024,512]{1,0:T(8,128)S(1)} %fusion.45) | copy-start | bytes 6291460
  73.1 28.0 %collective-permute-start.6 = (bf16[1,3,128,512]{3,2,1,0:T(8,128)(2,1)}, bf16[1,3,128,512]{3,2,1,0:T(8,128)(2,1)}, u32[]{:S(2)}, u32[]{:S(2)}) collective-permute-start(bf16[1,3,128,512]{3,2,1,0:T(8,128)(2,1)} %get-tuple-element.42), channel_id=1, source_target_pairs={{0,8},{8,16},{16,24},{24,32},{32,40},{40,48},{48,56},{56,64},{64,7... | collective-permute-start | bytes 1179656 | tf_op jit(solution)/shard_map/ppermute | solution.py:14
  77.6 23.6 %collective-permute-start.7 = (bf16[1,3,128,512]{3,2,1,0:T(8,128)(2,1)}, bf16[1,3,128,512]{3,2,1,0:T(8,128)(2,1)}, u32[]{:S(2)}, u32[]{:S(2)}) collective-permute-start(bf16[1,3,128,512]{3,2,1,0:T(8,128)(2,1)} %get-tuple-element.43), channel_id=1, source_target_pairs={{8,0},{16,8},{24,16},{32,24},{40,32},{48,40},{56,48},{64,56},{72,6... | collective-permute-start | bytes 1179656 | tf_op jit(solution)/shard_map/ppermute | solution.py:15
  177.5 14.9 %collective-permute-start.8 = (bf16[3,1,128,512]{3,2,1,0:T(8,128)(2,1)S(1)}, bf16[3,1,128,512]{3,2,1,0:T(8,128)(2,1)S(1)}, u32[]{:S(2)}, u32[]{:S(2)}) collective-permute-start(bf16[3,1,128,512]{3,2,1,0:T(8,128)(2,1)S(1)} %get-tuple-element.40), channel_id=1, source_target_pairs={{0,1},{1,2},{2,3},{3,4},{4,5},{5,6},{6,7},{7,0},{8,9},{9,10},{10,1... | collective-permute-start | bytes 1179656 | tf_op jit(solution)/shard_map/ppermute | solution.py:14
  177.5 13.1 %copy-start.14 = (bf16[1024,512]{1,0:T(8,128)(2,1)S(1)}, bf16[1024,512]{1,0:T(8,128)(2,1)}, u32[]{:S(2)}) copy-start(bf16[1024,512]{1,0:T(8,128)(2,1)} %param.23) | copy-start | bytes 3145732
  177.5 13.1 %copy-start.26 = (bf16[1024,512]{1,0:T(8,128)(2,1)S(1)}, bf16[1024,512]{1,0:T(8,128)(2,1)}, u32[]{:S(2)}) copy-start(bf16[1024,512]{1,0:T(8,128)(2,1)} %get-tuple-element.30) | copy-start | bytes 3145732
  177.5 14.8 %collective-permute-start.9 = (bf16[3,1,128,512]{3,2,1,0:T(8,128)(2,1)S(1)}, bf16[3,1,128,512]{3,2,1,0:T(8,128)(2,1)S(1)}, u32[]{:S(2)}, u32[]{:S(2)}) collective-permute-start(bf16[3,1,128,512]{3,2,1,0:T(8,128)(2,1)S(1)} %get-tuple-element.41), channel_id=1, source_target_pairs={{1,0},{2,1},{3,2},{4,3},{5,4},{6,5},{7,6},{0,7},{9,8},{10,9},{11,1... | collective-permute-start | bytes 1179656 | tf_op jit(solution)/shard_map/ppermute | solution.py:15
  192.8 9.7 %collective-permute-start.10 = (bf16[1,3,128,512]{3,2,1,0:T(8,128)(2,1)S(1)}, bf16[1,3,128,512]{3,2,1,0:T(8,128)(2,1)S(1)}, u32[]{:S(2)}, u32[]{:S(2)}) collective-permute-start(bf16[1,3,128,512]{3,2,1,0:T(8,128)(2,1)S(1)} %get-tuple-element.38), channel_id=1, source_target_pairs={{0,8},{8,16},{16,24},{24,32},{32,40},{40,48},{48,56},{56,64},{64,7... | collective-permute-start | bytes 1179656 | tf_op jit(solution)/shard_map/ppermute | solution.py:14
  197.1 9.4 %collective-permute-start.11 = (bf16[1,3,128,512]{3,2,1,0:T(8,128)(2,1)S(1)}, bf16[1,3,128,512]{3,2,1,0:T(8,128)(2,1)S(1)}, u32[]{:S(2)}, u32[]{:S(2)}) collective-permute-start(bf16[1,3,128,512]{3,2,1,0:T(8,128)(2,1)S(1)} %get-tuple-element.39), channel_id=1, source_target_pairs={{8,0},{16,8},{24,16},{32,24},{40,32},{48,40},{56,48},{64,56},{72,6... | collective-permute-start | bytes 1179656 | tf_op jit(solution)/shard_map/ppermute | solution.py:15
  206.8 11.1 %copy-start.32 = (bf16[64,512]{1,0:T(8,128)(2,1)S(1)}, bf16[64,512]{1,0:T(8,128)(2,1)}, u32[]{:S(2)}) copy-start(bf16[64,512]{1,0:T(8,128)(2,1)} %copy-done.31) | copy-start | bytes 196612
  206.8 12.4 %copy-start.38 = (f32[64,32]{1,0:T(8,128)S(1)}, f32[64,32]{1,0:T(8,128)}, u32[]{:S(2)}) copy-start(f32[64,32]{1,0:T(8,128)} %copy-done.37) | copy-start | bytes 24580
  247.6 9.3 %collective-permute-start.12 = (bf16[3,1,128,512]{3,2,1,0:T(8,128)(2,1)S(1)}, bf16[3,1,128,512]{3,2,1,0:T(8,128)(2,1)S(1)}, u32[]{:S(2)}, u32[]{:S(2)}) collective-permute-start(bf16[3,1,128,512]{3,2,1,0:T(8,128)(2,1)S(1)} %get-tuple-element.36), channel_id=1, source_target_pairs={{0,1},{1,2},{2,3},{3,4},{4,5},{5,6},{6,7},{7,0},{8,9},{9,10},{10,1... | collective-permute-start | bytes 1179656 | tf_op jit(solution)/shard_map/ppermute | solution.py:14
  252.2 7.5 %collective-permute-start.13 = (bf16[3,1,128,512]{3,2,1,0:T(8,128)(2,1)S(1)}, bf16[3,1,128,512]{3,2,1,0:T(8,128)(2,1)S(1)}, u32[]{:S(2)}, u32[]{:S(2)}) collective-permute-start(bf16[3,1,128,512]{3,2,1,0:T(8,128)(2,1)S(1)} %get-tuple-element.37), channel_id=1, source_target_pairs={{1,0},{2,1},{3,2},{4,3},{5,4},{6,5},{7,6},{0,7},{9,8},{10,9},{11,1... | collective-permute-start | bytes 1179656 | tf_op jit(solution)/shard_map/ppermute | solution.py:15
  261.4 14.7 %collective-permute-start.14 = (bf16[1,3,128,512]{3,2,1,0:T(8,128)(2,1)S(1)}, bf16[1,3,128,512]{3,2,1,0:T(8,128)(2,1)S(1)}, u32[]{:S(2)}, u32[]{:S(2)}) collective-permute-start(bf16[1,3,128,512]{3,2,1,0:T(8,128)(2,1)S(1)} %get-tuple-element.34), channel_id=1, source_target_pairs={{0,8},{8,16},{16,24},{24,32},{32,40},{40,48},{48,56},{56,64},{64,7... | collective-permute-start | bytes 1179656 | tf_op jit(solution)/shard_map/ppermute | solution.py:14
  264.6 15.9 %collective-permute-start.15 = (bf16[1,3,128,512]{3,2,1,0:T(8,128)(2,1)S(1)}, bf16[1,3,128,512]{3,2,1,0:T(8,128)(2,1)S(1)}, u32[]{:S(2)}, u32[]{:S(2)}) collective-permute-start(bf16[1,3,128,512]{3,2,1,0:T(8,128)(2,1)S(1)} %get-tuple-element.35), channel_id=1, source_target_pairs={{8,0},{16,8},{24,16},{32,24},{40,32},{48,40},{56,48},{64,56},{72,6... | collective-permute-start | bytes 1179656 | tf_op jit(solution)/shard_map/ppermute | solution.py:15
  (38 other events, 174.5 us)
Sparse Core Ops, SparseCore 0:
  244.8 173.2 all-reduce.2
where the time goes:
time: 441 us; the launch traced here: 435 us
  waiting for transfers between devices  169 us (38%)
  other arithmetic  106 us (24%)
  local copies, waits for them, and re-layouts  88.9 us (20%)
  starting transfers between devices  30.3 us (7%)
  matrix products  25 us (6%)
  between operations  15.3 us (3%)
    psum x1, waiting for transfers between devices, body(): lax.psum((source_grad_enc, target_grad_enc, output_grad_enc, source_grad_...  124 us
    scatter-add x2, other arithmetic, backward_side(): jax.ops.segment_sum(d_before.reshape(-1, width).astype(jnp.float32), slot...  37.3 us
    gather x3, local copies, waits for them, and re-layouts, forward_side(): before = source_proj[slots] + target_proj[:, None, :]  32.4 us
    ppermute x8, waiting for transfers between devices, padded(): before = lax.ppermute(last, axis, up)  23.8 us
    ppermute x8, starting transfers between devices, padded(): before = lax.ppermute(last, axis, up)  23.4 us
    ppermute x8, waiting for transfers between devices, padded(): after = lax.ppermute(initial, axis, down)  20.8 us
    reduce_sum x2, other arithmetic, forward_side(): jnp.sum(jax.nn.silu(before) * weights[:, :, None], axis=1)  17.7 us
    reduce_sum x2, other arithmetic, backward_side(): jnp.sum(d_before, axis=1, dtype=jnp.float32).astype(jnp.bfloat16)  16.2 us
  transfers between devices with their start and end apart: 17, of which 13 were waited for; matrix products, arithmetic and copies ran while one was open for 15% of the time, Pallas kernels for 0%

commit v1 on v0

v1 whole, which is shorter than its diff:
```python
import functools

import jax
import jax.numpy as jnp
from jax import lax
from jax.experimental import pallas as pl
from jax.experimental.pallas import tpu as pltpu
from jax.sharding import PartitionSpec as P

D = 512
GD = 1024
MD = 64
KE = 32
KD = 3
CAP = 128
ROWS = CAP + 16
NEAR = 640
NB = 16
NM = 8
AXES = ("band", "mesh")
BF = jnp.bfloat16
F32 = jnp.float32
MIB = 1 << 20

NN = (((1,), (0,)), ((), ()))
NT = (((1,), (1,)), ((), ()))
TN = (((0,), (0,)), ((), ()))


def mm(a, b, dims=NN):
    return lax.dot_general(a, b, dims, preferred_element_type=F32)


def iota(shape, dim):
    return lax.broadcasted_iota(jnp.int32, shape, dim)


def one_hot(index, shape, dim):
    return jnp.where(iota(shape, dim) == index, 1.0, 0.0).astype(BF)


def call(body, outs, name, flops, scratch=(), vmem=28, smem_first=False, n_in=0):
    specs = None
    if smem_first:
        specs = [pl.BlockSpec(memory_space=pltpu.SMEM)] + [pl.BlockSpec(memory_space=pltpu.VMEM)] * (n_in - 1)
    kwargs = {} if specs is None else dict(in_specs=specs)
    return pl.pallas_call(
        body,
        out_shape=[jax.ShapeDtypeStruct(s, t) for s, t in outs],
        scratch_shapes=list(scratch),
        name=name,
        cost_estimate=pl.CostEstimate(flops=flops, bytes_accessed=4 * MIB, transcendentals=0),
        compiler_params=pltpu.CompilerParams(vmem_limit_bytes=vmem * MIB),
        **kwargs,
    )


def pick_rows(send_ref, table_ref, latent_ref, *outs):
    columns = send_ref[...].T
    table = table_ref[...].astype(F32)
    pad = jnp.zeros((16, D - CAP), BF)
    for e in range(3):
        hot = jnp.concatenate(
            [one_hot(columns[:, 3 * a + e : 3 * a + e + 1], (CAP, GD), 1) for a in range(3)], axis=0
        )
        rows = mm(hot, latent_ref[...]).astype(BF)
        for a in range(3):
            i = 3 * a + e
            outs[e][a, 0:CAP, :] = rows[a * CAP : (a + 1) * CAP]
            numbers = jnp.where(iota((16, CAP), 0) == 0, table[i : i + 1, :], 0.0).astype(BF)
            outs[e][a, CAP:ROWS, :] = jnp.concatenate([numbers, pad], axis=1)


def sigmoid(v):
    return 0.5 * jnp.tanh(0.5 * v) + 0.5


def enc_forward(up, down, left, right, own, slot, count, latent, w_src, w_dst, w_out,
                mean_out, slope_out, new_out, table_out, recv_out, proj):
    for e in range(3):
        recv_out[e * CAP : (e + 1) * CAP] = up[e, 0:CAP]
        recv_out[(6 + e) * CAP : (7 + e) * CAP] = down[e, 0:CAP]
        table_out[e : e + 1] = up[e, CAP:ROWS, 0:CAP].astype(F32)[0:1]
        table_out[6 + e : 7 + e] = down[e, CAP:ROWS, 0:CAP].astype(F32)[0:1]
        side = (left, own, right)[e]
        recv_out[(3 + e) * CAP : (4 + e) * CAP] = side[1, 0:CAP]
        table_out[3 + e : 4 + e] = side[1, CAP:ROWS, 0:CAP].astype(F32)[0:1]
    table_out[9:16] = jnp.zeros((7, CAP), F32)
    for a in range(3):
        part = slice(a * 384, (a + 1) * 384)
        proj[part] = mm(recv_out[part], w_src[...]).astype(BF)
    columns = slot[...].T
    counts = jnp.broadcast_to(count[...], (8, MD)).T[:, 0:1]
    inverse = 1.0 / counts.astype(F32)
    target = mm(latent[...], w_dst[...])
    total = jnp.zeros((MD, D), F32)
    for c in range(4):
        hot = jnp.concatenate(
            [one_hot(columns[:, k : k + 1], (MD, 9 * CAP), 1) for k in range(8 * c, 8 * c + 8)], axis=0
        )
        values = mm(hot, proj[...])
        for j in range(8):
            k = 8 * c + j
            pre = values[j * MD : (j + 1) * MD] + target
            weight = jnp.where(k < counts, inverse, 0.0)
            sig = sigmoid(pre)
            act = pre * sig
            total = total + act * weight
            slope_out[k] = ((sig + act * (1.0 - sig)) * weight).astype(BF)
    mean = total.astype(BF)
    mean_out[...] = mean
    new_out[...] = (latent[...].astype(F32) + mm(mean, w_out[...])).astype(BF)


def merge_index(table, slot, count, out):
    numbers = table[...].astype(BF)
    for k in range(KD):
        s = slot[k : k + 1, :]
        high, low = s >> 7, s & 127
        found = mm(numbers, one_hot(low, (CAP, GD), 0))
        value = jnp.sum(jnp.where(iota((16, GD), 0) == high, found, 0.0), axis=0, keepdims=True)
        out[k : k + 1, :] = high * MD + value.astype(jnp.int32)
    out[3:4, :] = count[...]
    out[4:8, :] = jnp.zeros((4, GD), jnp.int32)


def decoder(up, own, down, index, grid, cot, w_src, w_dst, w_out,
            mean_out, dst_out, slots_out, back0, back1, back2, proj, acc):
    proj[0:192] = mm(up[...], w_src[...]).astype(BF)
    proj[192:384] = mm(own[...], w_src[...]).astype(BF)
    proj[384:576] = mm(down[...], w_src[...]).astype(BF)
    proj[576:NEAR] = jnp.zeros((NEAR - 576, D), BF)
    step = 256
    for g in range(0, GD, step):
        rows = index[:, g : g + step]
        columns = rows.T
        counts = columns[:, 3:4]
        inverse = 1.0 / counts.astype(F32)
        target = mm(grid[g : g + step], w_dst[...])
        upstream = mm(cot[g : g + step], w_out[...], NT)
        total = jnp.zeros((step, D), F32)
        received = jnp.zeros((step, D), F32)
        parts = []
        hot = jnp.concatenate([one_hot(columns[:, k : k + 1], (step, NEAR), 1) for k in range(KD)], axis=0)
        values = mm(hot, proj[...])
        for k in range(KD):
            pre = values[k * step : (k + 1) * step] + target
            weight = jnp.where(k < counts, inverse, 0.0)
            sig = sigmoid(pre)
            act = pre * sig
            total = total + act * weight
            change = (upstream * weight * (sig + act * (1.0 - sig))).astype(BF)
            received = received + change.astype(F32)
            parts.append(change)
        mean_out[g : g + step] = total.astype(BF)
        dst_out[g : g + step] = received.astype(BF)
        hot = jnp.concatenate([one_hot(rows[k : k + 1], (9 * MD, step), 0) for k in range(KD)], axis=1)
        added = mm(hot, jnp.concatenate(parts, axis=0))
        if g == 0:
            acc[...] = added
        else:
            acc[...] += added
    slots = acc[...].astype(BF)
    slots_out[...] = slots
    back = mm(slots, w_src[...], NT).astype(BF)
    for a in range(3):
        for e, ref in enumerate((back0, back1, back2)):
            ref[a] = back[(3 * a + e) * MD : (3 * a + e + 1) * MD]


def owner_chunk(place, half, one, two):
    core = place[0] ^ half
    x, y = place[1], place[2]
    first = jnp.where(core == 0, y, x)
    second = jnp.where(core == 0, x, y)
    number = core * 16 + ((first + one) & 3) * 4 + ((second + two) & 3)
    return pl.multiple_of(number * 16, 16)


def pack(place, grads, keep, send):
    for half, ref in enumerate((keep, send)):
        for one in range(4):
            for two in range(4):
                at = owner_chunk(place, half, one, two)
                for m in range(3):
                    ref[one, two, m] = grads[m, pl.ds(at, 16), :].astype(BF)


def dec_grads(place, up, own, down, slots, grid, dst, mean, cot, w_dst, keep, send, part_out, grads):
    grads[0] = (
        mm(up[...], slots[0:192], TN) + mm(own[...], slots[192:384], TN) + mm(down[...], slots[384:576], TN)
    )
    grads[1] = mm(grid[...], dst[...], TN)
    grads[2] = mm(mean[...], cot[...], TN)
    pack(place, grads, keep, send)
    for g in range(0, GD, 256):
        part_out[g : g + 256] = cot[g : g + 256].astype(F32) + mm(dst[g : g + 256], w_dst[...], NT)


def enc_backward(up, own, down, slope, row, w_src, w_dst, w_out,
                 grad_out, dround_out, dst_out, slots_out, back0, back1, back2, change):
    total = up[...].astype(F32) + own[...].astype(F32) + down[...].astype(F32)
    rounded = total.astype(BF)
    dround_out[...] = rounded
    upstream = mm(rounded, w_out[...], NT)
    received = jnp.zeros((MD, D), F32)
    for k in range(KE):
        value = (upstream * slope[k].astype(F32)).astype(BF)
        change[k * MD : (k + 1) * MD] = value
        received = received + value.astype(F32)
    dst = received.astype(BF)
    dst_out[...] = dst
    for e, ref in enumerate((back0, back1, back2)):
        hot = jnp.concatenate(
            [one_hot(row[...] - (3 * a + e) * CAP, (CAP, KE * MD), 0) for a in range(3)], axis=0
        )
        slots = mm(hot, change[...]).astype(BF)
        back = mm(slots, w_src[...], NT).astype(BF)
        for a in range(3):
            i = 3 * a + e
            slots_out[i * CAP : (i + 1) * CAP] = slots[a * CAP : (a + 1) * CAP]
            ref[a] = back[a * CAP : (a + 1) * CAP]
    grad_out[...] = total + mm(dst, w_dst[...], NT)


def enc_grads(place, recv, slots, latent, dst, mean, dround, keep, send, grads):
    grads[0] = mm(recv[...], slots[...], TN)
    grads[1] = mm(latent[...], dst[...], TN)
    grads[2] = mm(mean[...], dround[...], TN)
    pack(place, grads, keep, send)


def put_rows(send, up, left, own, right, down, part, out):
    for g in range(0, GD, 256):
        hot = jnp.concatenate(
            [one_hot(send[i : i + 1, :] - g, (256, CAP), 0) for i in range(9)], axis=1
        )
        rows = [up[e] for e in range(3)] + [left[1], own[1], right[1]] + [down[e] for e in range(3)]
        out[g : g + 256] = part[g : g + 256] + mm(hot, jnp.concatenate(rows, axis=0))


def unpack(place, mine, other, *outs):
    for half, ref in enumerate((mine, other)):
        for one in range(4):
            for two in range(4):
                at = owner_chunk(place, half, -one, -two)
                for m in range(3):
                    outs[m][pl.ds(at, 16), :] = ref[one, two, m].astype(F32)


def mesh_shift(x, by):
    return lax.ppermute(x, "mesh", [(i, (i + by) % NM) for i in range(NM)])


def band_shift(x, by):
    return lax.ppermute(x, "band", [(i, i + by) for i in range(NB) if 0 <= i + by < NB])


def device(x, y, z, core):
    return (x * 4 + z) * NM + y * 2 + core


def torus_shift(x, stage, by):
    pairs = []
    for i in range(NB * NM):
        b, j = divmod(i, NM)
        at = [b // 4, j // 2, b % 4]
        core = j % 2
        axis = {1: 1 - core, 2: core, 3: 2}[stage]
        to = list(at)
        to[axis] = (to[axis] + by) % 4
        pairs.append((i, device(*to, core)))
    return lax.ppermute(x, AXES, pairs)


def core_swap(x):
    pairs = [(i, i ^ 1) for i in range(NB * NM)]
    return lax.ppermute(x, AXES, pairs)


def add(*values):
    total = values[0].astype(F32)
    for v in values[1:]:
        total = total + v.astype(F32)
    return total.astype(BF)


def all_sum(keep, send):
    got = core_swap(send)
    s = [add(keep[d], got[d]) for d in range(4)]
    got = [torus_shift(s[d], 1, d) for d in (1, 2, 3)]
    s = [add(s[0][d], *(g[d] for g in got)) for d in range(4)]
    got = [torus_shift(s[d], 2, d) for d in (1, 2, 3)]
    v = add(s[0], *got)
    one, two, three = (torus_shift(v, 3, d) for d in (1, 2, 3))
    v = ((v.astype(F32) + two.astype(F32)) + (one.astype(F32) + three.astype(F32))).astype(BF)
    v = jnp.stack([v] + [torus_shift(v, 2, d) for d in (1, 2, 3)])
    v = jnp.stack([v] + [torus_shift(v, 1, d) for d in (1, 2, 3)])
    return v, core_swap(v)


def exchange(x0, x1, x2):
    left = mesh_shift(x2, 1)
    right = mesh_shift(x0, -1)
    up = band_shift(jnp.stack([left[2], x1[2], right[2]]), 1)
    down = band_shift(jnp.stack([left[0], x1[0], right[0]]), -1)
    return up, left, right, down


def body(grid_latent, mesh_latent, w_src_enc, w_dst_enc, w_out_enc, w_src_dec, w_dst_dec, w_out_dec, grid_cot,
         enc_send, enc_slot, enc_count, dec_send, dec_slot, dec_count):
    b, j = lax.axis_index("band"), lax.axis_index("mesh")
    place = jnp.stack([j % 2, b // 4, j // 2, b % 4]).astype(jnp.int32)
    send_index = jnp.pad(enc_send.reshape(9, CAP), ((0, 7), (0, 0)))
    send_table = jnp.pad(dec_send.reshape(9, CAP), ((0, 7), (0, 0)))
    slot_rows = enc_slot.T
    slot_line = slot_rows.reshape(1, KE * MD)

    block = ((3, ROWS, D), BF)
    x0, x1, x2 = call(pick_rows, [block] * 3, "pick_rows", 1300000000)(send_index, send_table, grid_latent)
    up, left, right, down = exchange(x0, x1, x2)
    mean_enc, slope, mesh_new, table, recv = call(
        enc_forward,
        [((MD, D), BF), ((KE, MD, D), BF), ((MD, D), BF), ((16, CAP), F32), ((9 * CAP, D), BF)],
        "enc_forward", 3400000000, scratch=[pltpu.VMEM((9 * CAP, D), BF)],
    )(up, down, left, right, x1, slot_rows, enc_count.reshape(1, MD), mesh_latent, w_src_enc, w_dst_enc, w_out_enc)

    up = band_shift(mesh_new, 1)
    down = band_shift(mesh_new, -1)
    (index,) = call(merge_index, [((8, GD), jnp.int32)], "merge_index", 100000000)(
        table, dec_slot.T, dec_count.reshape(1, GD)
    )
    mine = jnp.stack([up, mesh_new, down])
    left = mesh_shift(mine, 1)
    right = mesh_shift(mine, -1)
    near = [jnp.concatenate([left[a], mine[a], right[a]], axis=0) for a in range(3)]

    rows = ((GD, D), BF)
    mean_dec, dst_dec, slots_dec, b0, b1, b2 = call(
        decoder,
        [rows, rows, ((9 * MD, D), BF)] + [((3, MD, D), BF)] * 3,
        "decoder", 5500000000,
        scratch=[pltpu.VMEM((NEAR, D), BF), pltpu.VMEM((9 * MD, D), F32)],
    )(*near, index, grid_latent, grid_cot, w_src_dec, w_dst_dec, w_out_dec)

    left = mesh_shift(b2, 1)
    right = mesh_shift(b0, -1)
    sums = [left[a].astype(F32) + b1[a].astype(F32) + right[a].astype(F32) for a in range(3)]
    up = band_shift(sums[2].astype(BF), 1)
    down = band_shift(sums[0].astype(BF), -1)

    half = ((4, 4, 3, 16, D), BF)
    keep, send, grid_part = call(
        dec_grads, [half, half, ((GD, D), F32)], "dec_grads", 2300000000,
        scratch=[pltpu.VMEM((3, D, D), F32)], smem_first=True, n_in=10,
    )(place, *near, slots_dec, grid_latent, dst_dec, mean_dec, grid_cot, w_dst_dec)

    mesh_grad, dround, dst_enc, slots_enc, x0, x1, x2 = call(
        enc_backward,
        [((MD, D), F32), ((MD, D), BF), ((MD, D), BF), ((9 * CAP, D), BF)] + [((3, CAP, D), BF)] * 3,
        "enc_backward", 3200000000, scratch=[pltpu.VMEM((KE * MD, D), BF)],
    )(up, sums[1], down, slope, slot_line, w_src_enc, w_dst_enc, w_out_enc)
    keep_enc, send_enc = call(
        enc_grads, [half, half], "enc_grads", 700000000, scratch=[pltpu.VMEM((3, D, D), F32)],
        smem_first=True, n_in=7,
    )(place, recv, slots_enc, mesh_latent, dst_enc, mean_enc, dround)

    up, left, right, down = exchange(x0, x1, x2)
    (grid_grad,) = call(put_rows, [((GD, D), F32)], "put_rows", 1300000000)(
        send_index, up, left, x1, right, down, grid_part
    )
    square = ((D, D), F32)
    spread = functools.partial(call, unpack, [square] * 3, smem_first=True, n_in=3)
    dec = spread("unpack_dec", 1000000)(place, *all_sum(keep, send))
    enc = spread("unpack_enc", 1000000)(place, *all_sum(keep_enc, send_enc))
    return (grid_grad, mesh_grad, *enc, *dec)


def solution(mesh):
    rows = P(AXES, None)
    whole = P()
    return jax.shard_map(
        body,
        mesh=mesh,
        in_specs=(rows, rows) + (whole,) * 6 + (rows, P(AXES, None, None, None), rows, P(AXES),
                                               P(AXES, None, None, None), rows, P(AXES)),
        out_specs=(rows, rows) + (whole,) * 6,
        check_vma=False,
    )
```

time: 441 us -> 193 us (0.44); the launches traced: 435 us -> 193 us
  waiting for transfers between devices: 169 us -> 50.5 us
  other arithmetic: 106 us -> 4.06 us
  local copies, waits for them, and re-layouts: 88.9 us -> 10.1 us
  starting transfers between devices: 30.3 us -> 94.1 us
  Pallas kernels: 0 us -> 32.7 us
  matrix products: 25 us -> 0 us
  between operations: 15.3 us -> 1.22 us
    psum x1 -> x0, waiting for transfers between devices: 124 us -> none  [body(): lax.psum((source_grad_enc, target_grad_enc, output_grad_enc, source_grad_...]
    ppermute x16 -> x50, starting transfers between devices: 30.3 us -> 94.1 us  [the longest x30 38.2 us: torus_shift(): return lax.ppermute(x, AXES, pairs)]
    scatter-add x4 -> x0, other arithmetic: 61 us -> none  [the longest x2 37.3 us: backward_side(): jax.ops.segment_sum(d_before.reshape(-1, width).astype(jnp.float32), slot...]
    gather x5 -> x0, local copies, waits for them, and re-layouts: 40.8 us -> none  [the longest x3 32.4 us: forward_side(): before = source_proj[slots] + target_proj[:, None, :]]
    reduce_sum x4 -> x0, other arithmetic: 33.9 us -> none  [the longest x2 17.7 us: forward_side(): jnp.sum(jax.nn.silu(before) * weights[:, :, None], axis=1)]
    pallas_call x0 -> x10, Pallas kernels: none -> 32.7 us  [the longest x1 9.41 us: body(): call(decoder, [rows, rows, ((9 * MD, D), BF)] + [((3, MD, D), BF)] * 3, '...]
    dot_general x17 -> x0, matrix products: 25 us -> none  [the longest x2 4.98 us: backward_side(): jnp.dot(received.T, slot_sum, preferred_element_type=jnp.float32)]
    mul x2 -> x0, local copies, waits for them, and re-layouts: 15.5 us -> none  [backward_side(): upstream[:, None, :] * weights[:, :, None] * silu_slope(before)]
  transfers between devices with their start and end apart: 17 -> 50, of which waited for: 13 -> 20; matrix products, arithmetic and copies ran while one was open for 15% -> 1% of each run, Pallas kernels for 0% -> 8%
where the time goes in v1:
time: 193 us
  starting transfers between devices  94.1 us (49%)
  waiting for transfers between devices  50.5 us (26%)
  Pallas kernels  32.7 us (17%)
  local copies, waits for them, and re-layouts  10.1 us (5%)
  other arithmetic  4.06 us (2%)
    ppermute x30, starting transfers between devices, torus_shift(): return lax.ppermute(x, AXES, pairs)  38.2 us
    ppermute x8, starting transfers between devices, mesh_shift(): return lax.ppermute(x, 'mesh', [(i, (i + by) % NM) for i in range(NM)])  24.5 us
    ppermute x8, waiting for transfers between devices, band_shift(): lax.ppermute(x, 'band', [(i, i + by) for i in range(NB) if 0 <= i + by <...  20.5 us
    ppermute x8, starting transfers between devices, band_shift(): lax.ppermute(x, 'band', [(i, i + by) for i in range(NB) if 0 <= i + by <...  19.2 us
    ppermute x30, waiting for transfers between devices, torus_shift(): return lax.ppermute(x, AXES, pairs)  18.2 us
    ppermute x4, starting transfers between devices, core_swap(): return lax.ppermute(x, AXES, pairs)  12.2 us
    ppermute x8, waiting for transfers between devices, mesh_shift(): return lax.ppermute(x, 'mesh', [(i, (i + by) % NM) for i in range(NM)])  11.8 us
    unnamed x54, local copies, waits for them, and re-layouts  9.85 us
  transfers between devices with their start and end apart: 50, of which 20 were waited for; matrix products, arithmetic and copies ran while one was open for 1% of the time, Pallas kernels for 8%

profile of v1, /device:TPU:1, one launch (start us, length us, event | category | flops | bytes accessed | tf_op | source)
XLA Modules:
  0.0 192.7 jit_solution(15478847607711369395)
XLA Ops:
  7.7 6.2 %collective-permute-done.1.right = bf16[3,144,512]{2,1,0:T(8,128)(2,1)S(1)} collective-permute-done((bf16[3,144,512]{2,1,0:T(8,128)(2,1)S(1)}, bf16[3,144,512]{2,1,0:T(8,128)(2,1)S(1)}, u32[]{:S(2)}, u32[]{:S(2)}) %collective-permute-start.1) | collective-permute-done | bytes 442400 | tf_op jit(solution)/shard_map/ppermute | solution.py:252
  14.0 3.6 %collective-permute-start.2 = (bf16[3,144,512]{2,1,0:T(8,128)(2,1)S(1)}, bf16[3,144,512]{2,1,0:T(8,128)(2,1)S(1)}, u32[]{:S(2)}, u32[]{:S(2)}) collective-permute-start(bf16[3,144,512]{2,1,0:T(8,128)(2,1)S(1)} %pad_maximum_fusion.2), channel_id=1, source_target_pairs={{0,8},{8,16},{16,24},{24,32},{32,40},{40,48},{48,56},{56,64},{64,7... | collective-permute-start | bytes 1327112 | tf_op jit(solution)/shard_map/ppermute | solution.py:256
  19.0 4.2 %collective-permute-done.2.up = bf16[3,144,512]{2,1,0:T(8,128)(2,1)S(1)} collective-permute-done((bf16[3,144,512]{2,1,0:T(8,128)(2,1)S(1)}, bf16[3,144,512]{2,1,0:T(8,128)(2,1)S(1)}, u32[]{:S(2)}, u32[]{:S(2)}) %collective-permute-start.2) | collective-permute-done | bytes 442400 | tf_op jit(solution)/shard_map/ppermute | solution.py:256
  23.1 4.2 %collective-permute-done.3.down = bf16[3,144,512]{2,1,0:T(8,128)(2,1)S(1)} collective-permute-done((bf16[3,144,512]{2,1,0:T(8,128)(2,1)S(1)}, bf16[3,144,512]{2,1,0:T(8,128)(2,1)S(1)}, u32[]{:S(2)}, u32[]{:S(2)}) %collective-permute-start.3) | collective-permute-done | bytes 442400 | tf_op jit(solution)/shard_map/ppermute | solution.py:256
  27.5 4.4 %enc_forward.1 = (bf16[64,512]{1,0:T(8,128)(2,1)S(1)}, bf16[32,64,512]{2,1,0:T(8,128)(2,1)S(1)}, bf16[64,512]{1,0:T(8,128)(2,1)S(1)}, f32[16,128]{1,0:T(8,128)S(1)}, bf16[1152,512]{1,0:T(8,128)(2,1)S(1)}) custom-call(bf16[3,144,512]{2,1,0:T(8,128)(2,1)S(1)} %collective-permute-done.2.up, bf16[3,144,512]{2,1,0:T(8,128)(2,1)S(1)} %collective-permute-done.3.down, ...), custom_call_target="tpu_custom_call" | custom-call | flops 3400000000 | bytes 4194304 | tf_op jit(solution)/shard_map/enc_forward/pallas_call | solution.py:322
  33.5 4.2 %collective-permute-start.4 = (bf16[64,512]{1,0:T(8,128)(2,1)S(1)}, bf16[64,512]{1,0:T(8,128)(2,1)S(1)}, u32[]{:S(2)}, u32[]{:S(2)}) collective-permute-start(bf16[64,512]{1,0:T(8,128)(2,1)S(1)} %get-tuple-element.43), channel_id=1, source_target_pairs={{0,8},{8,16},{16,24},{24,32},{32,40},{40,48},{48,56},{56,64},{64,7... | collective-permute-start | bytes 196616 | tf_op jit(solution)/shard_map/ppermute | solution.py:256
  38.8 6.1 %collective-permute-start.7 = (bf16[3,64,512]{2,1,0:T(8,128)(2,1)S(1)}, bf16[3,64,512]{2,1,0:T(8,128)(2,1)S(1)}, u32[]{:S(2)}, u32[]{:S(2)}) collective-permute-start(bf16[3,64,512]{2,1,0:T(8,128)(2,1)S(1)} %pad_maximum_fusion.6), channel_id=1, source_target_pairs={{0,7},{1,0},{2,1},{3,2},{4,3},{5,4},{6,5},{7,6},{8,15},{9,8},{10,9... | collective-permute-start | bytes 589832 | tf_op jit(solution)/shard_map/ppermute | solution.py:252
  46.2 3.1 %collective-permute-done.7 = bf16[3,64,512]{2,1,0:T(8,128)(2,1)S(1)} collective-permute-done((bf16[3,64,512]{2,1,0:T(8,128)(2,1)S(1)}, bf16[3,64,512]{2,1,0:T(8,128)(2,1)S(1)}, u32[]{:S(2)}, u32[]{:S(2)}) %collective-permute-start.7) | collective-permute-done | bytes 196640 | tf_op jit(solution)/shard_map/ppermute | solution.py:252
  49.5 9.4 %decoder.1 = (bf16[1024,512]{1,0:T(8,128)(2,1)S(1)}, bf16[1024,512]{1,0:T(8,128)(2,1)S(1)}, bf16[576,512]{1,0:T(8,128)(2,1)S(1)}, bf16[3,64,512]{2,1,0:T(8,128)(...) custom-call(bf16[192,512]{1,0:T(8,128)(2,1)S(1)} %get-tuple-element.111.up, ...), custom_call_target="tpu_custom_call" | custom-call | flops 5500000256 | bytes 4194304 | tf_op jit(solution)/shard_map/decoder/pallas_call | solution.py:339
  61.7 4.3 %collective-permute-start.9 = (bf16[3,64,512]{2,1,0:T(8,128)(2,1)}, bf16[3,64,512]{2,1,0:T(8,128)(2,1)}, u32[]{:S(2)}, u32[]{:S(2)}) collective-permute-start(bf16[3,64,512]{2,1,0:T(8,128)(2,1)} %get-tuple-element.47), channel_id=1, source_target_pairs={{0,7},{1,0},{2,1},{3,2},{4,3},{5,4},{6,5},{7,6},{8,15},{9,8},{10,9... | collective-permute-start | bytes 589832 | tf_op jit(solution)/shard_map/ppermute | solution.py:252
  69.6 3.7 %collective-permute-start.10 = (bf16[64,512]{1,0:T(8,128)(2,1)S(1)}, bf16[64,512]{1,0:T(8,128)(2,1)S(1)}, u32[]{:S(2)}, u32[]{:S(2)}) collective-permute-start(bf16[64,512]{1,0:T(8,128)(2,1)S(1)} %get-tuple-element.88), channel_id=1, source_target_pairs={{0,8},{8,16},{16,24},{24,32},{32,40},{40,48},{48,56},{56,64},{64,7... | collective-permute-start | bytes 196616 | tf_op jit(solution)/shard_map/ppermute | solution.py:256
  80.4 3.0 %dec_grads.1 = (bf16[4,4,3,16,512]{4,3,2,1,0:T(8,128)(2,1)S(1)}, bf16[4,4,3,16,512]{4,3,2,1,0:T(8,128)(2,1)S(1)}, f32[1024,512]{1,0:T(8,128)S(1)}) custom-call(s32[4]{0:T(128)S(1)} %pad_add_fusion.place, bf16[192,512]{1,0:T(8,128)(2,1)S(1)} %get-tuple-element.111.up, bf16[192,512]{1,0:T(8,128)(2,1)S(1)} %get-tuple-element.112.own, ...), custom_call_target="tpu_custom_call" | custom-call | flops 2300000000 | bytes 4194304 | tf_op jit(solution)/shard_map/dec_grads/pallas_call | solution.py:353
  83.5 4.4 %collective-permute-start.33 = (bf16[4,4,3,16,512]{4,3,2,1,0:T(8,128)(2,1)S(1)}, bf16[4,4,3,16,512]{4,3,2,1,0:T(8,128)(2,1)S(1)}, u32[]{:S(2)}, u32[]{:S(2)}) collective-permute-start(bf16[4,4,3,16,512]{4,3,2,1,0:T(8,128)(2,1)S(1)} %get-tuple-element.68), channel_id=1, source_target_pairs={{0,1},{1,0},{2,3},{3,2},{4,5},{5,4},{6,7},{7,6},{8,9},{9,8},{10,11... | collective-permute-start | bytes 2359304 | tf_op jit(solution)/shard_map/ppermute | solution.py:278
  87.9 4.6 %enc_backward.1 = (f32[64,512]{1,0:T(8,128)}, bf16[64,512]{1,0:T(8,128)(2,1)S(1)}, bf16[64,512]{1,0:T(8,128)(2,1)S(1)}, bf16[1152,512]{1,0:T(8,128)(2,1)S(1)}, b...) custom-call(bf16[64,512]{1,0:T(8,128)(2,1)S(1)} %collective-permute-done.10.up, ...), custom_call_target="tpu_custom_call" | custom-call | flops 3200000000 | bytes 4194304 | tf_op jit(solution)/shard_map/enc_backward/pallas_call | solution.py:358
  95.2 12.1 %collective-permute-start.36 = (bf16[4,3,16,512]{3,2,1,0:T(8,128)(2,1)S(1)}, bf16[4,3,16,512]{3,2,1,0:T(8,128)(2,1)S(1)}, u32[]{:S(2)}, u32[]{:S(2)}) collective-permute-start(bf16[4,3,16,512]{3,2,1,0:T(8,128)(2,1)S(1)} %get-tuple-element.73), channel_id=1, source_target_pairs={{0,6},{1,97},{2,0},{3,99},{4,2},{5,101},{6,4},{7,103},{8,14},{9,10... | collective-permute-start | bytes 589832 | tf_op jit(solution)/shard_map/ppermute | solution.py:273
  137.5 3.0 %collective-permute-start.48 = (bf16[4,3,16,512]{3,2,1,0:T(8,128)(2,1)S(1)}, bf16[4,3,16,512]{3,2,1,0:T(8,128)(2,1)S(1)}, u32[]{:S(2)}, u32[]{:S(2)}) collective-permute-start(bf16[4,3,16,512]{3,2,1,0:T(8,128)(2,1)S(1)} %get-tuple-element.102), channel_id=1, source_target_pairs={{0,6},{1,97},{2,0},{3,99},{4,2},{5,101},{6,4},{7,103},{8,14},{9,10... | collective-permute-start | bytes 589832 | tf_op jit(solution)/shard_map/ppermute | solution.py:273
  142.3 2.9 %collective-permute-done.27 = bf16[3,16,512]{2,1,0:T(8,128)(2,1)S(1)} collective-permute-done((bf16[3,16,512]{2,1,0:T(8,128)(2,1)S(1)}, bf16[3,16,512]{2,1,0:T(8,128)(2,1)S(1)}, u32[]{:S(2)}, u32[]{:S(2)}) %collective-permute-start.27) | collective-permute-done | bytes 49184 | tf_op jit(solution)/shard_map/ppermute | solution.py:273
  145.1 9.8 %collective-permute-start.12 = (bf16[3,128,512]{2,1,0:T(8,128)(2,1)S(1)}, bf16[3,128,512]{2,1,0:T(8,128)(2,1)S(1)}, u32[]{:S(2)}, u32[]{:S(2)}) collective-permute-start(bf16[3,128,512]{2,1,0:T(8,128)(2,1)S(1)} %get-tuple-element.49), channel_id=1, source_target_pairs={{0,1},{1,2},{2,3},{3,4},{4,5},{5,6},{6,7},{7,0},{8,9},{9,10},{10,1... | collective-permute-start | bytes 1179656 | tf_op jit(solution)/shard_map/ppermute | solution.py:252
  155.0 2.7 %collective-permute-start.31 = (bf16[4,3,16,512]{3,2,1,0:T(8,128)(2,1)S(1)}, bf16[4,3,16,512]{3,2,1,0:T(8,128)(2,1)S(1)}, u32[]{:S(2)}, u32[]{:S(2)}) collective-permute-start(bf16[4,3,16,512]{3,2,1,0:T(8,128)(2,1)S(1)} %get-tuple-element.104), channel_id=1, source_target_pairs={{0,6},{1,97},{2,0},{3,99},{4,2},{5,101},{6,4},{7,103},{8,14},{9,10... | collective-permute-start | bytes 589832 | tf_op jit(solution)/shard_map/ppermute | solution.py:273
  161.1 3.6 %collective-permute-start.49 = (bf16[4,4,3,16,512]{4,3,2,1,0:T(8,128)(2,1)S(1)}, bf16[4,4,3,16,512]{4,3,2,1,0:T(8,128)(2,1)S(1)}, u32[]{:S(2)}, u32[]{:S(2)}) collective-permute-start(bf16[4,4,3,16,512]{4,3,2,1,0:T(8,128)(2,1)S(1)} %pad_maximum_fusion.1.mine), channel_id=1, source_target_pairs={{0,1},{1,0},{2,3},{3,2},{4,5},{5,4},{6,7},{7,6},{8,9},{9,8},{10,11... | collective-permute-start | bytes 2359304 | tf_op jit(solution)/shard_map/ppermute | solution.py:278
  166.1 4.1 %collective-permute-start.32 = (bf16[4,4,3,16,512]{4,3,2,1,0:T(8,128)(2,1)S(1)}, bf16[4,4,3,16,512]{4,3,2,1,0:T(8,128)(2,1)S(1)}, u32[]{:S(2)}, u32[]{:S(2)}) collective-permute-start(bf16[4,4,3,16,512]{4,3,2,1,0:T(8,128)(2,1)S(1)} %pad_maximum_fusion.mine), channel_id=1, source_target_pairs={{0,1},{1,0},{2,3},{3,2},{4,5},{5,4},{6,7},{7,6},{8,9},{9,8},{10,11... | collective-permute-start | bytes 2359304 | tf_op jit(solution)/shard_map/ppermute | solution.py:278
  173.9 7.1 %collective-permute-done.14.up = bf16[3,128,512]{2,1,0:T(8,128)(2,1)S(1)} collective-permute-done((bf16[3,128,512]{2,1,0:T(8,128)(2,1)S(1)}, bf16[3,128,512]{2,1,0:T(8,128)(2,1)S(1)}, u32[]{:S(2)}, u32[]{:S(2)}) %collective-permute-start.14) | collective-permute-done | bytes 393248 | tf_op jit(solution)/shard_map/ppermute | solution.py:256
  181.1 3.9 %collective-permute-done.15.down = bf16[3,128,512]{2,1,0:T(8,128)(2,1)S(1)} collective-permute-done((bf16[3,128,512]{2,1,0:T(8,128)(2,1)S(1)}, bf16[3,128,512]{2,1,0:T(8,128)(2,1)S(1)}, u32[]{:S(2)}, u32[]{:S(2)}) %collective-permute-start.15) | collective-permute-done | bytes 393248 | tf_op jit(solution)/shard_map/ppermute | solution.py:256
  184.9 2.9 %put_rows.1 = f32[1024,512]{1,0:T(8,128)} custom-call(s32[16,128]{1,0:T(8,128)S(1)} %pad.7.send_ref.send, bf16[3,128,512]{2,1,0:T(8,128)(2,1)S(1)} %collective-permute-done.14.up, bf16[3,128,512]{2,1,0:T(8,128)(2,1)S(1)} %collective-permute-done.12.left, bf16[3,128,512]{2,1,0:T(8,128)(2,1)S(1)} %get-tuple-element.50.own, ...), custom_call_target="tpu_custom_call" | custom-call | flops 1300000000 | bytes 4194304 | tf_op jit(solution)/shard_map/put_rows/pallas_call | solution.py:369
  (176 shorter events, 74.0 us)
Async XLA Ops:
  4.9 9.0 %collective-permute-start.1 = (bf16[3,144,512]{2,1,0:T(8,128)(2,1)S(1)}, bf16[3,144,512]{2,1,0:T(8,128)(2,1)S(1)}, u32[]{:S(2)}, u32[]{:S(2)}) collective-permute-start(bf16[3,144,512]{2,1,0:T(8,128)(2,1)S(1)} %get-tuple-element.42), channel_id=1, source_target_pairs={{0,7},{1,0},{2,1},{3,2},{4,3},{5,4},{6,5},{7,6},{8,15},{9,8},{10,9... | collective-permute-start | bytes 1327112 | tf_op jit(solution)/shard_map/ppermute | solution.py:252
  6.4 7.6 %collective-permute-start = (bf16[3,144,512]{2,1,0:T(8,128)(2,1)S(1)}, bf16[3,144,512]{2,1,0:T(8,128)(2,1)S(1)}, u32[]{:S(2)}, u32[]{:S(2)}) collective-permute-start(bf16[3,144,512]{2,1,0:T(8,128)(2,1)S(1)} %get-tuple-element.40), channel_id=1, source_target_pairs={{0,1},{1,2},{2,3},{3,4},{4,5},{5,6},{6,7},{7,0},{8,9},{9,10},{10,1... | collective-permute-start | bytes 1327112 | tf_op jit(solution)/shard_map/ppermute | solution.py:252
  14.0 9.1 %collective-permute-start.2 = (bf16[3,144,512]{2,1,0:T(8,128)(2,1)S(1)}, bf16[3,144,512]{2,1,0:T(8,128)(2,1)S(1)}, u32[]{:S(2)}, u32[]{:S(2)}) collective-permute-start(bf16[3,144,512]{2,1,0:T(8,128)(2,1)S(1)} %pad_maximum_fusion.2), channel_id=1, source_target_pairs={{0,8},{8,16},{16,24},{24,32},{32,40},{40,48},{48,56},{56,64},{64,7... | collective-permute-start | bytes 1327112 | tf_op jit(solution)/shard_map/ppermute | solution.py:256
  17.7 9.7 %collective-permute-start.3 = (bf16[3,144,512]{2,1,0:T(8,128)(2,1)S(1)}, bf16[3,144,512]{2,1,0:T(8,128)(2,1)S(1)}, u32[]{:S(2)}, u32[]{:S(2)}) collective-permute-start(bf16[3,144,512]{2,1,0:T(8,128)(2,1)S(1)} %pad_maximum_fusion.3), channel_id=1, source_target_pairs={{8,0},{16,8},{24,16},{32,24},{40,32},{48,40},{56,48},{64,56},{72,6... | collective-permute-start | bytes 1327112 | tf_op jit(solution)/shard_map/ppermute | solution.py:256
  38.8 10.5 %collective-permute-start.7 = (bf16[3,64,512]{2,1,0:T(8,128)(2,1)S(1)}, bf16[3,64,512]{2,1,0:T(8,128)(2,1)S(1)}, u32[]{:S(2)}, u32[]{:S(2)}) collective-permute-start(bf16[3,64,512]{2,1,0:T(8,128)(2,1)S(1)} %pad_maximum_fusion.6), channel_id=1, source_target_pairs={{0,7},{1,0},{2,1},{3,2},{4,3},{5,4},{6,5},{7,6},{8,15},{9,8},{10,9... | collective-permute-start | bytes 589832 | tf_op jit(solution)/shard_map/ppermute | solution.py:252
  69.6 18.2 %collective-permute-start.10 = (bf16[64,512]{1,0:T(8,128)(2,1)S(1)}, bf16[64,512]{1,0:T(8,128)(2,1)S(1)}, u32[]{:S(2)}, u32[]{:S(2)}) collective-permute-start(bf16[64,512]{1,0:T(8,128)(2,1)S(1)} %get-tuple-element.88), channel_id=1, source_target_pairs={{0,8},{8,16},{16,24},{24,32},{32,40},{40,48},{48,56},{56,64},{64,7... | collective-permute-start | bytes 196616 | tf_op jit(solution)/shard_map/ppermute | solution.py:256
  73.3 14.5 %collective-permute-start.11 = (bf16[64,512]{1,0:T(8,128)(2,1)S(1)}, bf16[64,512]{1,0:T(8,128)(2,1)S(1)}, u32[]{:S(2)}, u32[]{:S(2)}) collective-permute-start(bf16[64,512]{1,0:T(8,128)(2,1)S(1)} %get-tuple-element.86), channel_id=1, source_target_pairs={{8,0},{16,8},{24,16},{32,24},{40,32},{48,40},{56,48},{64,56},{72,6... | collective-permute-start | bytes 196616 | tf_op jit(solution)/shard_map/ppermute | solution.py:256
  83.5 11.4 %collective-permute-start.33 = (bf16[4,4,3,16,512]{4,3,2,1,0:T(8,128)(2,1)S(1)}, bf16[4,4,3,16,512]{4,3,2,1,0:T(8,128)(2,1)S(1)}, u32[]{:S(2)}, u32[]{:S(2)}) collective-permute-start(bf16[4,4,3,16,512]{4,3,2,1,0:T(8,128)(2,1)S(1)} %get-tuple-element.68), channel_id=1, source_target_pairs={{0,1},{1,0},{2,3},{3,2},{4,5},{5,4},{6,7},{7,6},{8,9},{9,8},{10,11... | collective-permute-start | bytes 2359304 | tf_op jit(solution)/shard_map/ppermute | solution.py:278
  94.3 13.7 %collective-permute-start.16 = (bf16[4,4,3,16,512]{4,3,2,1,0:T(8,128)(2,1)S(1)}, bf16[4,4,3,16,512]{4,3,2,1,0:T(8,128)(2,1)S(1)}, u32[]{:S(2)}, u32[]{:S(2)}) collective-permute-start(bf16[4,4,3,16,512]{4,3,2,1,0:T(8,128)(2,1)S(1)} %get-tuple-element.63), channel_id=1, source_target_pairs={{0,1},{1,0},{2,3},{3,2},{4,5},{5,4},{6,7},{7,6},{8,9},{9,8},{10,11... | collective-permute-start | bytes 2359304 | tf_op jit(solution)/shard_map/ppermute | solution.py:278
  94.4 60.6 %collective-permute-start.13 = (bf16[3,128,512]{2,1,0:T(8,128)(2,1)S(1)}, bf16[3,128,512]{2,1,0:T(8,128)(2,1)S(1)}, u32[]{:S(2)}, u32[]{:S(2)}) collective-permute-start(bf16[3,128,512]{2,1,0:T(8,128)(2,1)S(1)} %get-tuple-element.51), channel_id=1, source_target_pairs={{0,7},{1,0},{2,1},{3,2},{4,3},{5,4},{6,5},{7,6},{8,15},{9,8},{10,9... | collective-permute-start | bytes 1179656 | tf_op jit(solution)/shard_map/ppermute | solution.py:252
  95.2 16.8 %collective-permute-start.36 = (bf16[4,3,16,512]{3,2,1,0:T(8,128)(2,1)S(1)}, bf16[4,3,16,512]{3,2,1,0:T(8,128)(2,1)S(1)}, u32[]{:S(2)}, u32[]{:S(2)}) collective-permute-start(bf16[4,3,16,512]{3,2,1,0:T(8,128)(2,1)S(1)} %get-tuple-element.73), channel_id=1, source_target_pairs={{0,6},{1,97},{2,0},{3,99},{4,2},{5,101},{6,4},{7,103},{8,14},{9,10... | collective-permute-start | bytes 589832 | tf_op jit(solution)/shard_map/ppermute | solution.py:273
  107.4 8.6 %collective-permute-start.34 = (bf16[4,3,16,512]{3,2,1,0:T(8,128)(2,1)S(1)}, bf16[4,3,16,512]{3,2,1,0:T(8,128)(2,1)S(1)}, u32[]{:S(2)}, u32[]{:S(2)}) collective-permute-start(bf16[4,3,16,512]{3,2,1,0:T(8,128)(2,1)S(1)} %get-tuple-element.75), channel_id=1, source_target_pairs={{0,2},{1,33},{2,4},{3,35},{4,6},{5,37},{6,0},{7,39},{8,10},{9,41},... | collective-permute-start | bytes 589832 | tf_op jit(solution)/shard_map/ppermute | solution.py:273
  108.3 7.9 %collective-permute-start.19 = (bf16[4,3,16,512]{3,2,1,0:T(8,128)(2,1)S(1)}, bf16[4,3,16,512]{3,2,1,0:T(8,128)(2,1)S(1)}, u32[]{:S(2)}, u32[]{:S(2)}) collective-permute-start(bf16[4,3,16,512]{3,2,1,0:T(8,128)(2,1)S(1)} %get-tuple-element.77), channel_id=1, source_target_pairs={{0,6},{1,97},{2,0},{3,99},{4,2},{5,101},{6,4},{7,103},{8,14},{9,10... | collective-permute-start | bytes 589832 | tf_op jit(solution)/shard_map/ppermute | solution.py:273
  133.2 8.2 %collective-permute-start.28 = (bf16[3,16,512]{2,1,0:T(8,128)(2,1)S(1)}, bf16[3,16,512]{2,1,0:T(8,128)(2,1)S(1)}, u32[]{:S(2)}, u32[]{:S(2)}) collective-permute-start(bf16[3,16,512]{2,1,0:T(8,128)(2,1)S(1)} %add_convert_fusion.11), channel_id=1, source_target_pairs={{0,96},{1,7},{2,98},{3,1},{4,100},{5,3},{6,102},{7,5},{8,104},{9,1... | collective-permute-start | bytes 147464 | tf_op jit(solution)/shard_map/ppermute | solution.py:273
  137.5 20.2 %collective-permute-start.48 = (bf16[4,3,16,512]{3,2,1,0:T(8,128)(2,1)S(1)}, bf16[4,3,16,512]{3,2,1,0:T(8,128)(2,1)S(1)}, u32[]{:S(2)}, u32[]{:S(2)}) collective-permute-start(bf16[4,3,16,512]{3,2,1,0:T(8,128)(2,1)S(1)} %get-tuple-element.102), channel_id=1, source_target_pairs={{0,6},{1,97},{2,0},{3,99},{4,2},{5,101},{6,4},{7,103},{8,14},{9,10... | collective-permute-start | bytes 589832 | tf_op jit(solution)/shard_map/ppermute | solution.py:273
  140.5 17.3 %collective-permute-start.47 = (bf16[4,3,16,512]{3,2,1,0:T(8,128)(2,1)S(1)}, bf16[4,3,16,512]{3,2,1,0:T(8,128)(2,1)S(1)}, u32[]{:S(2)}, u32[]{:S(2)}) collective-permute-start(bf16[4,3,16,512]{3,2,1,0:T(8,128)(2,1)S(1)} %get-tuple-element.102), channel_id=1, source_target_pairs={{0,4},{1,65},{2,6},{3,67},{4,0},{5,69},{6,2},{7,71},{8,12},{9,73},... | collective-permute-start | bytes 589832 | tf_op jit(solution)/shard_map/ppermute | solution.py:273
  141.5 13.5 %collective-permute-start.26 = (bf16[3,16,512]{2,1,0:T(8,128)(2,1)S(1)}, bf16[3,16,512]{2,1,0:T(8,128)(2,1)S(1)}, u32[]{:S(2)}, u32[]{:S(2)}) collective-permute-start(bf16[3,16,512]{2,1,0:T(8,128)(2,1)S(1)} %add_convert_fusion.11), channel_id=1, source_target_pairs={{0,32},{1,3},{2,34},{3,5},{4,36},{5,7},{6,38},{7,1},{8,40},{9,11},... | collective-permute-start | bytes 147464 | tf_op jit(solution)/shard_map/ppermute | solution.py:273
  145.1 25.1 %collective-permute-start.12 = (bf16[3,128,512]{2,1,0:T(8,128)(2,1)S(1)}, bf16[3,128,512]{2,1,0:T(8,128)(2,1)S(1)}, u32[]{:S(2)}, u32[]{:S(2)}) collective-permute-start(bf16[3,128,512]{2,1,0:T(8,128)(2,1)S(1)} %get-tuple-element.49), channel_id=1, source_target_pairs={{0,1},{1,2},{2,3},{3,4},{4,5},{5,6},{6,7},{7,0},{8,9},{9,10},{10,1... | collective-permute-start | bytes 1179656 | tf_op jit(solution)/shard_map/ppermute | solution.py:252
  155.0 9.7 %collective-permute-start.31 = (bf16[4,3,16,512]{3,2,1,0:T(8,128)(2,1)S(1)}, bf16[4,3,16,512]{3,2,1,0:T(8,128)(2,1)S(1)}, u32[]{:S(2)}, u32[]{:S(2)}) collective-permute-start(bf16[4,3,16,512]{3,2,1,0:T(8,128)(2,1)S(1)} %get-tuple-element.104), channel_id=1, source_target_pairs={{0,6},{1,97},{2,0},{3,99},{4,2},{5,101},{6,4},{7,103},{8,14},{9,10... | collective-permute-start | bytes 589832 | tf_op jit(solution)/shard_map/ppermute | solution.py:273
  157.8 8.2 %collective-permute-start.29 = (bf16[4,3,16,512]{3,2,1,0:T(8,128)(2,1)S(1)}, bf16[4,3,16,512]{3,2,1,0:T(8,128)(2,1)S(1)}, u32[]{:S(2)}, u32[]{:S(2)}) collective-permute-start(bf16[4,3,16,512]{3,2,1,0:T(8,128)(2,1)S(1)} %get-tuple-element.104), channel_id=1, source_target_pairs={{0,2},{1,33},{2,4},{3,35},{4,6},{5,37},{6,0},{7,39},{8,10},{9,41},... | collective-permute-start | bytes 589832 | tf_op jit(solution)/shard_map/ppermute | solution.py:273
  161.1 26.7 %collective-permute-start.49 = (bf16[4,4,3,16,512]{4,3,2,1,0:T(8,128)(2,1)S(1)}, bf16[4,4,3,16,512]{4,3,2,1,0:T(8,128)(2,1)S(1)}, u32[]{:S(2)}, u32[]{:S(2)}) collective-permute-start(bf16[4,4,3,16,512]{4,3,2,1,0:T(8,128)(2,1)S(1)} %pad_maximum_fusion.1.mine), channel_id=1, source_target_pairs={{0,1},{1,0},{2,3},{3,2},{4,5},{5,4},{6,7},{7,6},{8,9},{9,8},{10,11... | collective-permute-start | bytes 2359304 | tf_op jit(solution)/shard_map/ppermute | solution.py:278
  166.1 24.2 %collective-permute-start.32 = (bf16[4,4,3,16,512]{4,3,2,1,0:T(8,128)(2,1)S(1)}, bf16[4,4,3,16,512]{4,3,2,1,0:T(8,128)(2,1)S(1)}, u32[]{:S(2)}, u32[]{:S(2)}) collective-permute-start(bf16[4,4,3,16,512]{4,3,2,1,0:T(8,128)(2,1)S(1)} %pad_maximum_fusion.mine), channel_id=1, source_target_pairs={{0,1},{1,0},{2,3},{3,2},{4,5},{5,4},{6,7},{7,6},{8,9},{9,8},{10,11... | collective-permute-start | bytes 2359304 | tf_op jit(solution)/shard_map/ppermute | solution.py:278
  170.3 10.8 %collective-permute-start.14 = (bf16[3,128,512]{2,1,0:T(8,128)(2,1)S(1)}, bf16[3,128,512]{2,1,0:T(8,128)(2,1)S(1)}, u32[]{:S(2)}, u32[]{:S(2)}) collective-permute-start(bf16[3,128,512]{2,1,0:T(8,128)(2,1)S(1)} %pad_maximum_fusion.4), channel_id=1, source_target_pairs={{0,8},{8,16},{16,24},{24,32},{32,40},{40,48},{48,56},{56,64},{64,7... | collective-permute-start | bytes 1179656 | tf_op jit(solution)/shard_map/ppermute | solution.py:256
  172.6 12.3 %collective-permute-start.15 = (bf16[3,128,512]{2,1,0:T(8,128)(2,1)S(1)}, bf16[3,128,512]{2,1,0:T(8,128)(2,1)S(1)}, u32[]{:S(2)}, u32[]{:S(2)}) collective-permute-start(bf16[3,128,512]{2,1,0:T(8,128)(2,1)S(1)} %pad_maximum_fusion.5), channel_id=1, source_target_pairs={{8,0},{16,8},{24,16},{32,24},{40,32},{48,40},{56,48},{64,56},{72,6... | collective-permute-start | bytes 1179656 | tf_op jit(solution)/shard_map/ppermute | solution.py:256
  (53 other events, 455.6 us)

commit v2 on v1

--- a/solution.py
+++ b/solution.py
@@ -39,11 +39,24 @@
     return jnp.where(iota(shape, dim) == index, 1.0, 0.0).astype(BF)
 
 
-def call(body, outs, name, flops, scratch=(), vmem=28, smem_first=False, n_in=0):
-    specs = None
-    if smem_first:
-        specs = [pl.BlockSpec(memory_space=pltpu.SMEM)] + [pl.BlockSpec(memory_space=pltpu.VMEM)] * (n_in - 1)
-    kwargs = {} if specs is None else dict(in_specs=specs)
+def place():
+    b, j = lax.axis_index("band"), lax.axis_index("mesh")
+    return j & 1, b >> 2, j >> 1, b & 1
+
+
+def own_number(block):
+    core, _, _, odd = place()
+    a = (block * 11) >> 5
+    e = block - 3 * a
+    return 3 * jnp.where(odd == 1, 2 - a, a) + jnp.where(core == 1, 2 - e, e)
+
+
+def own_slot(slot):
+    return (own_number(slot >> 7) << 7) | (slot & 127)
+
+
+def call(body, outs, name, flops, scratch=(), vmem=28, in_place=False):
+    kwargs = dict(out_specs=[pl.BlockSpec(memory_space=pl.ANY)] * len(outs)) if in_place else {}
     return pl.pallas_call(
         body,
         out_shape=[jax.ShapeDtypeStruct(s, t) for s, t in outs],
@@ -55,9 +68,9 @@
     )
 
 
-def pick_rows(send_ref, table_ref, latent_ref, *outs):
-    columns = send_ref[...].T
-    table = table_ref[...].astype(F32)
+def pick_rows(send_ref, latent_ref, *outs):
+    columns = send_ref[0:16].T
+    table = send_ref[16:32].astype(F32)
     pad = jnp.zeros((16, D - CAP), BF)
     for e in range(3):
         hot = jnp.concatenate(
@@ -89,7 +102,7 @@
     for a in range(3):
         part = slice(a * 384, (a + 1) * 384)
         proj[part] = mm(recv_out[part], w_src[...]).astype(BF)
-    columns = slot[...].T
+    columns = own_slot(slot[...]).T
     counts = jnp.broadcast_to(count[...], (8, MD)).T[:, 0:1]
     inverse = 1.0 / counts.astype(F32)
     target = mm(latent[...], w_dst[...])
@@ -112,11 +125,14 @@
     new_out[...] = (latent[...].astype(F32) + mm(mean, w_out[...])).astype(BF)
 
 
-def merge_index(table, slot, count, out):
+def merge_index(table, slot, count, enc_slot, out, line_out):
+    own = own_slot(enc_slot[...])
+    for k in range(0, KE, 2):
+        line_out[:, k * MD : (k + 2) * MD] = jnp.concatenate([own[k : k + 1], own[k + 1 : k + 2]], axis=1)
     numbers = table[...].astype(BF)
     for k in range(KD):
         s = slot[k : k + 1, :]
-        high, low = s >> 7, s & 127
+        high, low = own_number(s >> 7), s & 127
         found = mm(numbers, one_hot(low, (CAP, GD), 0))
         value = jnp.sum(jnp.where(iota((16, GD), 0) == high, found, 0.0), axis=0, keepdims=True)
         out[k : k + 1, :] = high * MD + value.astype(jnp.int32)
@@ -168,31 +184,31 @@
             ref[a] = back[(3 * a + e) * MD : (3 * a + e + 1) * MD]
 
 
-def owner_chunk(place, half, one, two):
-    core = place[0] ^ half
-    x, y = place[1], place[2]
+def owner_chunk(half, one, two):
+    core, x, y, _ = place()
+    core = core ^ half
     first = jnp.where(core == 0, y, x)
     second = jnp.where(core == 0, x, y)
     number = core * 16 + ((first + one) & 3) * 4 + ((second + two) & 3)
     return pl.multiple_of(number * 16, 16)
 
 
-def pack(place, grads, keep, send):
+def pack(grads, keep, send):
     for half, ref in enumerate((keep, send)):
         for one in range(4):
             for two in range(4):
-                at = owner_chunk(place, half, one, two)
+                at = owner_chunk(half, one, two)
                 for m in range(3):
                     ref[one, two, m] = grads[m, pl.ds(at, 16), :].astype(BF)
 
 
-def dec_grads(place, up, own, down, slots, grid, dst, mean, cot, w_dst, keep, send, part_out, grads):
+def dec_grads(up, own, down, slots, grid, dst, mean, cot, w_dst, keep, send, part_out, grads):
     grads[0] = (
         mm(up[...], slots[0:192], TN) + mm(own[...], slots[192:384], TN) + mm(down[...], slots[384:576], TN)
     )
     grads[1] = mm(grid[...], dst[...], TN)
     grads[2] = mm(mean[...], cot[...], TN)
-    pack(place, grads, keep, send)
+    pack(grads, keep, send)
     for g in range(0, GD, 256):
         part_out[g : g + 256] = cot[g : g + 256].astype(F32) + mm(dst[g : g + 256], w_dst[...], NT)
 
@@ -210,9 +226,10 @@
         received = received + value.astype(F32)
     dst = received.astype(BF)
     dst_out[...] = dst
+    line = row[...]
     for e, ref in enumerate((back0, back1, back2)):
         hot = jnp.concatenate(
-            [one_hot(row[...] - (3 * a + e) * CAP, (CAP, KE * MD), 0) for a in range(3)], axis=0
+            [one_hot(line - (3 * a + e) * CAP, (CAP, KE * MD), 0) for a in range(3)], axis=0
         )
         slots = mm(hot, change[...]).astype(BF)
         back = mm(slots, w_src[...], NT).astype(BF)
@@ -223,11 +240,11 @@
     grad_out[...] = total + mm(dst, w_dst[...], NT)
 
 
-def enc_grads(place, recv, slots, latent, dst, mean, dround, keep, send, grads):
+def enc_grads(recv, slots, latent, dst, mean, dround, keep, send, grads):
     grads[0] = mm(recv[...], slots[...], TN)
     grads[1] = mm(latent[...], dst[...], TN)
     grads[2] = mm(mean[...], dround[...], TN)
-    pack(place, grads, keep, send)
+    pack(grads, keep, send)
 
 
 def put_rows(send, up, left, own, right, down, part, out):
@@ -239,21 +256,41 @@
         out[g : g + 256] = part[g : g + 256] + mm(hot, jnp.concatenate(rows, axis=0))
 
 
-def unpack(place, mine, other, *outs):
-    for half, ref in enumerate((mine, other)):
-        for one in range(4):
-            for two in range(4):
-                at = owner_chunk(place, half, -one, -two)
-                for m in range(3):
-                    outs[m][pl.ds(at, 16), :] = ref[one, two, m].astype(F32)
-
-
-def mesh_shift(x, by):
-    return lax.ppermute(x, "mesh", [(i, (i + by) % NM) for i in range(NM)])
-
-
-def band_shift(x, by):
-    return lax.ppermute(x, "band", [(i, i + by) for i in range(NB) if 0 <= i + by < NB])
+def unpack(mine, other, *refs):
+    outs, (whole, sems) = refs[:6], refs[6:]
+    copies = [pltpu.make_async_copy(whole.at[m], outs[m], sems.at[m]) for m in range(6)]
+    for m in range(6):
+        for half, ref in enumerate((mine, other)):
+            for one in range(4):
+                for two in range(4):
+                    whole[m, pl.ds(owner_chunk(half, -one, -two), 16), :] = ref[one, two, m].astype(F32)
+        copies[m].start()
+    for copy in copies:
+        copy.wait()
+
+
+def pairs(x, partner):
+    return lax.ppermute(x, AXES, [(i, partner(i)) for i in range(NB * NM) if partner(i) is not None])
+
+
+def other_core(x):
+    return pairs(x, lambda i: i ^ 1)
+
+
+def other_chip(x):
+    return pairs(x, lambda i: i // NM * NM + (i % NM + (1 if i % 2 else -1)) % NM)
+
+
+def near_band(x):
+    return pairs(x, lambda i: i ^ NM)
+
+
+def far_band(x):
+    def partner(i):
+        to = i + (NM if i // NM % 2 else -NM)
+        return to if 0 <= to < NB * NM else None
+
+    return pairs(x, partner)
 
 
 def device(x, y, z, core):
@@ -261,21 +298,14 @@
 
 
 def torus_shift(x, stage, by):
-    pairs = []
-    for i in range(NB * NM):
+    def partner(i):
         b, j = divmod(i, NM)
         at = [b // 4, j // 2, b % 4]
-        core = j % 2
-        axis = {1: 1 - core, 2: core, 3: 2}[stage]
-        to = list(at)
-        to[axis] = (to[axis] + by) % 4
-        pairs.append((i, device(*to, core)))
-    return lax.ppermute(x, AXES, pairs)
-
-
-def core_swap(x):
-    pairs = [(i, i ^ 1) for i in range(NB * NM)]
-    return lax.ppermute(x, AXES, pairs)
+        axis = {1: 1 - j % 2, 2: j % 2, 3: 2}[stage]
+        at[axis] = (at[axis] + by) % 4
+        return device(*at, j % 2)
+
+    return pairs(x, partner)
 
 
 def add(*values):
@@ -285,54 +315,63 @@
     return total.astype(BF)
 
 
-def all_sum(keep, send):
-    got = core_swap(send)
-    s = [add(keep[d], got[d]) for d in range(4)]
+def scatter_sum(*packed):
+    got = [other_core(send) for _, send in packed]
+    s = [jnp.concatenate([add(keep[d], g[d]) for (keep, _), g in zip(packed, got)], axis=1) for d in range(4)]
     got = [torus_shift(s[d], 1, d) for d in (1, 2, 3)]
-    s = [add(s[0][d], *(g[d] for g in got)) for d in range(4)]
+    return [add(s[0][d], *(g[d] for g in got)) for d in range(4)]
+
+
+def second_sum(s):
     got = [torus_shift(s[d], 2, d) for d in (1, 2, 3)]
-    v = add(s[0], *got)
+    return add(s[0], *got)
+
+
+def spread_sum(v):
     one, two, three = (torus_shift(v, 3, d) for d in (1, 2, 3))
     v = ((v.astype(F32) + two.astype(F32)) + (one.astype(F32) + three.astype(F32))).astype(BF)
     v = jnp.stack([v] + [torus_shift(v, 2, d) for d in (1, 2, 3)])
     v = jnp.stack([v] + [torus_shift(v, 1, d) for d in (1, 2, 3)])
-    return v, core_swap(v)
-
-
-def exchange(x0, x1, x2):
-    left = mesh_shift(x2, 1)
-    right = mesh_shift(x0, -1)
-    up = band_shift(jnp.stack([left[2], x1[2], right[2]]), 1)
-    down = band_shift(jnp.stack([left[0], x1[0], right[0]]), -1)
-    return up, left, right, down
+    return v, other_core(v)
+
+
+def first_exchange(x0, x1, x2):
+    return other_chip(x0), x1, other_core(x2)
+
+
+def second_exchange(left, own, right):
+    up = far_band(jnp.stack([left[0], own[0], right[0]]))
+    down = near_band(jnp.stack([left[2], own[2], right[2]]))
+    return up, down
 
 
 def body(grid_latent, mesh_latent, w_src_enc, w_dst_enc, w_out_enc, w_src_dec, w_dst_dec, w_out_dec, grid_cot,
          enc_send, enc_slot, enc_count, dec_send, dec_slot, dec_count):
-    b, j = lax.axis_index("band"), lax.axis_index("mesh")
-    place = jnp.stack([j % 2, b // 4, j // 2, b % 4]).astype(jnp.int32)
-    send_index = jnp.pad(enc_send.reshape(9, CAP), ((0, 7), (0, 0)))
-    send_table = jnp.pad(dec_send.reshape(9, CAP), ((0, 7), (0, 0)))
+    core, _, _, odd = place()
+    sends = jnp.concatenate([enc_send, dec_send], axis=0)
+    sends = jnp.where(odd == 1, sends[:, ::-1], sends)
+    sends = jnp.where(core == 1, sends[:, :, ::-1], sends)
+    sends = jnp.pad(sends.reshape(2, 9, CAP), ((0, 0), (0, 7), (0, 0))).reshape(32, CAP)
     slot_rows = enc_slot.T
-    slot_line = slot_rows.reshape(1, KE * MD)
 
     block = ((3, ROWS, D), BF)
-    x0, x1, x2 = call(pick_rows, [block] * 3, "pick_rows", 1300000000)(send_index, send_table, grid_latent)
-    up, left, right, down = exchange(x0, x1, x2)
+    x0, x1, x2 = call(pick_rows, [block] * 3, "pick_rows", 1300000000)(sends, grid_latent)
+    left, _, right = first_exchange(x0, x1, x2)
+    up, down = second_exchange(left, x1, right)
     mean_enc, slope, mesh_new, table, recv = call(
         enc_forward,
         [((MD, D), BF), ((KE, MD, D), BF), ((MD, D), BF), ((16, CAP), F32), ((9 * CAP, D), BF)],
         "enc_forward", 3400000000, scratch=[pltpu.VMEM((9 * CAP, D), BF)],
     )(up, down, left, right, x1, slot_rows, enc_count.reshape(1, MD), mesh_latent, w_src_enc, w_dst_enc, w_out_enc)
 
-    up = band_shift(mesh_new, 1)
-    down = band_shift(mesh_new, -1)
-    (index,) = call(merge_index, [((8, GD), jnp.int32)], "merge_index", 100000000)(
-        table, dec_slot.T, dec_count.reshape(1, GD)
-    )
+    up = far_band(mesh_new)
+    down = near_band(mesh_new)
+    index, slot_line = call(
+        merge_index, [((8, GD), jnp.int32), ((1, KE * MD), jnp.int32)], "merge_index", 100000000
+    )(table, dec_slot.T, dec_count.reshape(1, GD), slot_rows)
     mine = jnp.stack([up, mesh_new, down])
-    left = mesh_shift(mine, 1)
-    right = mesh_shift(mine, -1)
+    left = other_chip(mine)
+    right = other_core(mine)
     near = [jnp.concatenate([left[a], mine[a], right[a]], axis=0) for a in range(3)]
 
     rows = ((GD, D), BF)
@@ -343,37 +382,40 @@
         scratch=[pltpu.VMEM((NEAR, D), BF), pltpu.VMEM((9 * MD, D), F32)],
     )(*near, index, grid_latent, grid_cot, w_src_dec, w_dst_dec, w_out_dec)
 
-    left = mesh_shift(b2, 1)
-    right = mesh_shift(b0, -1)
+    left = other_chip(b0)
+    right = other_core(b2)
     sums = [left[a].astype(F32) + b1[a].astype(F32) + right[a].astype(F32) for a in range(3)]
-    up = band_shift(sums[2].astype(BF), 1)
-    down = band_shift(sums[0].astype(BF), -1)
+    up = far_band(sums[0].astype(BF))
+    down = near_band(sums[2].astype(BF))
 
     half = ((4, 4, 3, 16, D), BF)
-    keep, send, grid_part = call(
-        dec_grads, [half, half, ((GD, D), F32)], "dec_grads", 2300000000,
-        scratch=[pltpu.VMEM((3, D, D), F32)], smem_first=True, n_in=10,
-    )(place, *near, slots_dec, grid_latent, dst_dec, mean_dec, grid_cot, w_dst_dec)
+    *packed_dec, grid_part = call(
+        dec_grads, [half, half, ((GD, D), F32)], "dec_grads", 2300000000, scratch=[pltpu.VMEM((3, D, D), F32)],
+    )(*near, slots_dec, grid_latent, dst_dec, mean_dec, grid_cot, w_dst_dec)
 
     mesh_grad, dround, dst_enc, slots_enc, x0, x1, x2 = call(
         enc_backward,
         [((MD, D), F32), ((MD, D), BF), ((MD, D), BF), ((9 * CAP, D), BF)] + [((3, CAP, D), BF)] * 3,
         "enc_backward", 3200000000, scratch=[pltpu.VMEM((KE * MD, D), BF)],
     )(up, sums[1], down, slope, slot_line, w_src_enc, w_dst_enc, w_out_enc)
-    keep_enc, send_enc = call(
+    packed_enc = call(
         enc_grads, [half, half], "enc_grads", 700000000, scratch=[pltpu.VMEM((3, D, D), F32)],
-        smem_first=True, n_in=7,
-    )(place, recv, slots_enc, mesh_latent, dst_enc, mean_enc, dround)
-
-    up, left, right, down = exchange(x0, x1, x2)
+    )(recv, slots_enc, mesh_latent, dst_enc, mean_enc, dround)
+
+    left, _, right = first_exchange(x0, x1, x2)
+    part_sums = scatter_sum(packed_enc, packed_dec)
+    part_sums, left, right = lax.optimization_barrier((part_sums, left, right))
+    up, down = second_exchange(left, x1, right)
+    part_sum = second_sum(part_sums)
+    part_sum, up, down = lax.optimization_barrier((part_sum, up, down))
     (grid_grad,) = call(put_rows, [((GD, D), F32)], "put_rows", 1300000000)(
-        send_index, up, left, x1, right, down, grid_part
+        sends, up, left, x1, right, down, grid_part
     )
-    square = ((D, D), F32)
-    spread = functools.partial(call, unpack, [square] * 3, smem_first=True, n_in=3)
-    dec = spread("unpack_dec", 1000000)(place, *all_sum(keep, send))
-    enc = spread("unpack_enc", 1000000)(place, *all_sum(keep_enc, send_enc))
-    return (grid_grad, mesh_grad, *enc, *dec)
+    grads = call(
+        unpack, [((D, D), F32)] * 6, "unpack", 1000000,
+        scratch=[pltpu.VMEM((6, D, D), F32), pltpu.SemaphoreType.DMA((6,))], in_place=True,
+    )(*spread_sum(part_sum))
+    return (grid_grad, mesh_grad, *grads)
 
 
 def solution(mesh):

time: 193 us -> 161 us (0.83)
  starting transfers between devices: 94.1 us -> 76.5 us
  local copies, waits for them, and re-layouts: 10.1 us -> 1.46 us
  Pallas kernels: 32.7 us -> 28.8 us
    ppermute x50 -> x34, starting transfers between devices: 94.1 us -> 76.5 us  [pairs(): lax.ppermute(x, AXES, [(i, partner(i)) for i in range(NB * NM) if partner...]
    unnamed x54 -> x28, local copies, waits for them, and re-layouts: 9.85 us -> 1.3 us
    pallas_call x4 -> x3, Pallas kernels: 6.59 us -> 4.6 us  [the longest x1 2.85 us: body(): call(unpack, [((D, D), F32)] * 6, 'unpack', 1000000, scratch=[pltpu.VMEM(...]
    ppermute x50 -> x34, waiting for transfers between devices: 50.5 us -> 50.7 us  [pairs(): lax.ppermute(x, AXES, [(i, partner(i)) for i in range(NB * NM) if partner...]
  transfers between devices with their start and end apart: 50 -> 34, of which waited for: 20 -> 21; matrix products, arithmetic and copies ran while one was open for 1% -> 1% of each run, Pallas kernels for 8% -> 7%
where the time goes in v2:
time: 161 us
  starting transfers between devices  76.5 us (48%)
  waiting for transfers between devices  50.7 us (31%)
  Pallas kernels  28.8 us (18%)
  other arithmetic  2.42 us (2%)
    ppermute x34, starting transfers between devices, pairs(): lax.ppermute(x, AXES, [(i, partner(i)) for i in range(NB * NM) if partner...  76.5 us
    ppermute x34, waiting for transfers between devices, pairs(): lax.ppermute(x, AXES, [(i, partner(i)) for i in range(NB * NM) if partner...  50.7 us
    pallas_call x1, Pallas kernels, body(): call(decoder, [rows, rows, ((9 * MD, D), BF)] + [((3, MD, D), BF)] * 3, '...  8.76 us
    pallas_call x1, Pallas kernels, body(): call(enc_backward, [((MD, D), F32), ((MD, D), BF), ((MD, D), BF), ((9 * C...  4.55 us
    pallas_call x1, Pallas kernels, body(): call(enc_forward, [((MD, D), BF), ((KE, MD, D), BF), ((MD, D), BF), ((16,...  4.36 us
  transfers between devices with their start and end apart: 34, of which 21 were waited for; matrix products, arithmetic and copies ran while one was open for 1% of the time, Pallas kernels for 7%

profile of v2, /device:TPU:1, one launch (start us, length us, event | category | flops | bytes accessed | tf_op | source)
XLA Modules:
  0.0 161.2 jit_solution(11396430464051054101)
XLA Ops:
  8.3 4.9 %collective-permute-done.left = bf16[3,144,512]{2,1,0:T(8,128)(2,1)S(1)} collective-permute-done((bf16[3,144,512]{2,1,0:T(8,128)(2,1)S(1)}, bf16[3,144,512]{2,1,0:T(8,128)(2,1)S(1)}, u32[]{:S(2)}, u32[]{:S(2)}) %collective-permute-start) | collective-permute-done | bytes 442400 | tf_op jit(solution)/shard_map/ppermute | solution.py:273
  14.1 4.6 %collective-permute-start.3 = (bf16[3,144,512]{2,1,0:T(8,128)(2,1)S(1)}, bf16[3,144,512]{2,1,0:T(8,128)(2,1)S(1)}, u32[]{:S(2)}, u32[]{:S(2)}) collective-permute-start(bf16[3,144,512]{2,1,0:T(8,128)(2,1)S(1)} %pad_maximum_fusion.2), channel_id=1, source_target_pairs={{0,8},{1,9},{2,10},{3,11},{4,12},{5,13},{6,14},{7,15},{8,0},{9,1},... | collective-permute-start | bytes 1327112 | tf_op jit(solution)/shard_map/ppermute | solution.py:273
  18.7 8.7 %collective-permute-done.3.down = bf16[3,144,512]{2,1,0:T(8,128)(2,1)S(1)} collective-permute-done((bf16[3,144,512]{2,1,0:T(8,128)(2,1)S(1)}, bf16[3,144,512]{2,1,0:T(8,128)(2,1)S(1)}, u32[]{:S(2)}, u32[]{:S(2)}) %collective-permute-start.3) | collective-permute-done | bytes 442400 | tf_op jit(solution)/shard_map/ppermute | solution.py:273
  27.5 4.4 %enc_forward.1 = (bf16[64,512]{1,0:T(8,128)(2,1)S(1)}, bf16[32,64,512]{2,1,0:T(8,128)(2,1)S(1)}, bf16[64,512]{1,0:T(8,128)(2,1)S(1)}, f32[16,128]{1,0:T(8,128)S(1)}, bf16[1152,512]{1,0:T(8,128)(2,1)S(1)}) custom-call(bf16[3,144,512]{2,1,0:T(8,128)(2,1)S(1)} %collective-permute-done.2.up, bf16[3,144,512]{2,1,0:T(8,128)(2,1)S(1)} %collective-permute-done.3.down, ...), custom_call_target="tpu_custom_call" | custom-call | flops 3400000000 | bytes 4194304 | tf_op jit(solution)/shard_map/enc_forward/pallas_call | solution.py:361
  35.1 3.6 %collective-permute-start.7 = (bf16[3,64,512]{2,1,0:T(8,128)(2,1)S(1)}, bf16[3,64,512]{2,1,0:T(8,128)(2,1)S(1)}, u32[]{:S(2)}, u32[]{:S(2)}) collective-permute-start(bf16[3,64,512]{2,1,0:T(8,128)(2,1)S(1)} %pad_maximum_fusion.9), channel_id=1, source_target_pairs={{0,1},{1,0},{2,3},{3,2},{4,5},{5,4},{6,7},{7,6},{8,9},{9,8},{10,11... | collective-permute-start | bytes 589832 | tf_op jit(solution)/shard_map/ppermute | solution.py:273
  40.3 4.3 %collective-permute-done.6 = bf16[3,64,512]{2,1,0:T(8,128)(2,1)S(1)} collective-permute-done((bf16[3,64,512]{2,1,0:T(8,128)(2,1)S(1)}, bf16[3,64,512]{2,1,0:T(8,128)(2,1)S(1)}, u32[]{:S(2)}, u32[]{:S(2)}) %collective-permute-start.6) | collective-permute-done | bytes 196640 | tf_op jit(solution)/shard_map/ppermute | solution.py:273
  44.8 8.8 %decoder.1 = (bf16[1024,512]{1,0:T(8,128)(2,1)S(1)}, bf16[1024,512]{1,0:T(8,128)(2,1)S(1)}, bf16[576,512]{1,0:T(8,128)(2,1)S(1)}, bf16[3,64,512]{2,1,0:T(8,128)(...) custom-call(bf16[192,512]{1,0:T(8,128)(2,1)S(1)} %get-tuple-element.128.up, ...), custom_call_target="tpu_custom_call" | custom-call | flops 5500000256 | bytes 4194304 | tf_op jit(solution)/shard_map/decoder/pallas_call | solution.py:378
  54.4 3.9 %collective-permute-start.9 = (bf16[3,64,512]{2,1,0:T(8,128)(2,1)S(1)}, bf16[3,64,512]{2,1,0:T(8,128)(2,1)S(1)}, u32[]{:S(2)}, u32[]{:S(2)}) collective-permute-start(bf16[3,64,512]{2,1,0:T(8,128)(2,1)S(1)} %get-tuple-element.60), channel_id=1, source_target_pairs={{0,1},{1,0},{2,3},{3,2},{4,5},{5,4},{6,7},{7,6},{8,9},{9,8},{10,11... | collective-permute-start | bytes 589832 | tf_op jit(solution)/shard_map/ppermute | solution.py:273
  59.5 5.3 %collective-permute-start.11 = (bf16[64,512]{1,0:T(8,128)(2,1)S(1)}, bf16[64,512]{1,0:T(8,128)(2,1)S(1)}, u32[]{:S(2)}, u32[]{:S(2)}) collective-permute-start(bf16[64,512]{1,0:T(8,128)(2,1)S(1)} %get-tuple-element.105), channel_id=1, source_target_pairs={{0,8},{1,9},{2,10},{3,11},{4,12},{5,13},{6,14},{7,15},{8,0},{9,1},... | collective-permute-start | bytes 196616 | tf_op jit(solution)/shard_map/ppermute | solution.py:273
  67.8 2.9 %collective-permute-start.13 = (bf16[4,4,3,16,512]{4,3,2,1,0:T(8,128)(2,1)S(1)}, bf16[4,4,3,16,512]{4,3,2,1,0:T(8,128)(2,1)S(1)}, u32[]{:S(2)}, u32[]{:S(2)}) collective-permute-start(bf16[4,4,3,16,512]{4,3,2,1,0:T(8,128)(2,1)S(1)} %get-tuple-element.73), channel_id=1, source_target_pairs={{0,1},{1,0},{2,3},{3,2},{4,5},{5,4},{6,7},{7,6},{8,9},{9,8},{10,11... | collective-permute-start | bytes 2359304 | tf_op jit(solution)/shard_map/ppermute | solution.py:273
  70.7 4.5 %enc_backward.1 = (f32[64,512]{1,0:T(8,128)}, bf16[64,512]{1,0:T(8,128)(2,1)S(1)}, bf16[64,512]{1,0:T(8,128)(2,1)S(1)}, bf16[1152,512]{1,0:T(8,128)(2,1)S(1)}, b...) custom-call(bf16[64,512]{1,0:T(8,128)(2,1)S(1)} %collective-permute-done.10.up, ...), custom_call_target="tpu_custom_call" | custom-call | flops 3200000000 | bytes 4194304 | tf_op jit(solution)/shard_map/enc_backward/pallas_call | solution.py:396
  79.3 8.2 %collective-permute-start.15 = (bf16[4,6,16,512]{3,2,1,0:T(8,128)(2,1)S(1)}, bf16[4,6,16,512]{3,2,1,0:T(8,128)(2,1)S(1)}, u32[]{:S(2)}, u32[]{:S(2)}) collective-permute-start(bf16[4,6,16,512]{3,2,1,0:T(8,128)(2,1)S(1)} %pad_maximum_fusion.4), channel_id=1, source_target_pairs={{0,4},{1,65},{2,6},{3,67},{4,0},{5,69},{6,2},{7,71},{8,12},{9,73},... | collective-permute-start | bytes 1179656 | tf_op jit(solution)/shard_map/ppermute | solution.py:273
  92.7 4.8 %collective-permute-done.16 = bf16[4,6,16,512]{3,2,1,0:T(8,128)(2,1)S(1)} collective-permute-done((bf16[4,6,16,512]{3,2,1,0:T(8,128)(2,1)S(1)}, bf16[4,6,16,512]{3,2,1,0:T(8,128)(2,1)S(1)}, u32[]{:S(2)}, u32[]{:S(2)}) %collective-permute-start.16) | collective-permute-done | bytes 393248 | tf_op jit(solution)/shard_map/ppermute | solution.py:273
  98.6 5.6 %collective-permute-start.23 = (bf16[3,128,512]{2,1,0:T(8,128)(2,1)S(1)}, bf16[3,128,512]{2,1,0:T(8,128)(2,1)S(1)}, u32[]{:S(2)}, u32[]{:S(2)}) collective-permute-start(bf16[3,128,512]{2,1,0:T(8,128)(2,1)S(1)} %pad_maximum_fusion.7), channel_id=1, source_target_pairs={{0,8},{1,9},{2,10},{3,11},{4,12},{5,13},{6,14},{7,15},{8,0},{9,1},... | collective-permute-start | bytes 1179656 | tf_op jit(solution)/shard_map/ppermute | solution.py:273
  104.2 3.1 %collective-permute-start.20 = (bf16[6,16,512]{2,1,0:T(8,128)(2,1)S(1)}, bf16[6,16,512]{2,1,0:T(8,128)(2,1)S(1)}, u32[]{:S(2)}, u32[]{:S(2)}) collective-permute-start(bf16[6,16,512]{2,1,0:T(8,128)(2,1)S(1)} %get-tuple-element.78), channel_id=1, source_target_pairs={{0,64},{1,5},{2,66},{3,7},{4,68},{5,1},{6,70},{7,3},{8,72},{9,13},... | collective-permute-start | bytes 294920 | tf_op jit(solution)/shard_map/ppermute | solution.py:273
  111.7 4.9 %collective-permute-start.26 = (bf16[6,16,512]{2,1,0:T(8,128)(2,1)S(1)}, bf16[6,16,512]{2,1,0:T(8,128)(2,1)S(1)}, u32[]{:S(2)}, u32[]{:S(2)}) collective-permute-start(bf16[6,16,512]{2,1,0:T(8,128)(2,1)S(1)} %add_convert_fusion.9), channel_id=1, source_target_pairs={{0,24},{1,25},{2,26},{3,27},{4,28},{5,29},{6,30},{7,31},{8,0},{9,1... | collective-permute-start | bytes 294920 | tf_op jit(solution)/shard_map/ppermute | solution.py:273
  118.2 4.1 %collective-permute-done.25 = bf16[6,16,512]{2,1,0:T(8,128)(2,1)S(1)} collective-permute-done((bf16[6,16,512]{2,1,0:T(8,128)(2,1)S(1)}, bf16[6,16,512]{2,1,0:T(8,128)(2,1)S(1)}, u32[]{:S(2)}, u32[]{:S(2)}) %collective-permute-start.25) | collective-permute-done | bytes 98336 | tf_op jit(solution)/shard_map/ppermute | solution.py:273
  122.4 3.7 %collective-permute-start.29 = (bf16[6,16,512]{2,1,0:T(8,128)(2,1)S(1)}, bf16[6,16,512]{2,1,0:T(8,128)(2,1)S(1)}, u32[]{:S(2)}, u32[]{:S(2)}) collective-permute-start(bf16[6,16,512]{2,1,0:T(8,128)(2,1)S(1)} %add_convert_fusion.8), channel_id=1, source_target_pairs={{0,96},{1,7},{2,98},{3,1},{4,100},{5,3},{6,102},{7,5},{8,104},{9,1... | collective-permute-start | bytes 294920 | tf_op jit(solution)/shard_map/ppermute | solution.py:273
  131.9 2.9 %collective-permute-start.31 = (bf16[4,6,16,512]{3,2,1,0:T(8,128)(2,1)S(1)}, bf16[4,6,16,512]{3,2,1,0:T(8,128)(2,1)S(1)}, u32[]{:S(2)}, u32[]{:S(2)}) collective-permute-start(bf16[4,6,16,512]{3,2,1,0:T(8,128)(2,1)S(1)} %get-tuple-element.115), channel_id=1, source_target_pairs={{0,4},{1,65},{2,6},{3,67},{4,0},{5,69},{6,2},{7,71},{8,12},{9,73},... | collective-permute-start | bytes 1179656 | tf_op jit(solution)/shard_map/ppermute | solution.py:273
  137.4 3.8 %collective-permute-done.31 = bf16[4,6,16,512]{3,2,1,0:T(8,128)(2,1)S(1)} collective-permute-done((bf16[4,6,16,512]{3,2,1,0:T(8,128)(2,1)S(1)}, bf16[4,6,16,512]{3,2,1,0:T(8,128)(2,1)S(1)}, u32[]{:S(2)}, u32[]{:S(2)}) %collective-permute-start.31) | collective-permute-done | bytes 393248 | tf_op jit(solution)/shard_map/ppermute | solution.py:273
  141.2 4.3 %collective-permute-done.30 = bf16[4,6,16,512]{3,2,1,0:T(8,128)(2,1)S(1)} collective-permute-done((bf16[4,6,16,512]{3,2,1,0:T(8,128)(2,1)S(1)}, bf16[4,6,16,512]{3,2,1,0:T(8,128)(2,1)S(1)}, u32[]{:S(2)}, u32[]{:S(2)}) %collective-permute-start.30) | collective-permute-done | bytes 393248 | tf_op jit(solution)/shard_map/ppermute | solution.py:273
  145.7 9.4 %collective-permute-start.33 = (bf16[4,4,6,16,512]{4,3,2,1,0:T(8,128)(2,1)S(1)}, bf16[4,4,6,16,512]{4,3,2,1,0:T(8,128)(2,1)S(1)}, u32[]{:S(2)}, u32[]{:S(2)}) collective-permute-start(bf16[4,4,6,16,512]{4,3,2,1,0:T(8,128)(2,1)S(1)} %pad_maximum_fusion.mine), channel_id=1, source_target_pairs={{0,1},{1,0},{2,3},{3,2},{4,5},{5,4},{6,7},{7,6},{8,9},{9,8},{10,11... | collective-permute-start | bytes 4718600 | tf_op jit(solution)/shard_map/ppermute | solution.py:273
  155.1 2.8 %put_rows.1 = f32[1024,512]{1,0:T(8,128)} custom-call(s32[32,128]{1,0:T(8,128)S(1)} %bitcast.62, bf16[3,128,512]{2,1,0:T(8,128)(2,1)S(1)} %collective-permute-done.22.up, bf16[3,128,512]{2,1,0:T(8,128)(2,1)S(1)} %collective-permute-done.17.left, bf16[3,128,512]{2,1,0:T(8,128)(2,1)S(1)} %get-tuple-element.81.own, ...), custom_call_target="tpu_custom_call" | custom-call | flops 1300000000 | bytes 4194304 | tf_op jit(solution)/shard_map/put_rows/pallas_call | solution.py:411
  158.1 2.9 %unpack.1 = (f32[512,512]{1,0:T(8,128)}, f32[512,512]{1,0:T(8,128)}, f32[512,512]{1,0:T(8,128)}, f32[512,512]{1,0:T(8,128)}, f32[512,512]{1,0:T(8,128)}, /*index=5*/f32[512,512]{1,0:T(8,128)}) custom-call(bf16[4,4,6,16,512]{4,3,2,1,0:T(8,128)(2,1)S(1)} %pad_maximum_fusion.mine, bf16[4,4,6,16,512]{4,3,2,1,0:T(8,128)(2,1)S(1)} %collective-permute-done.33.other), custom_call_target="tpu_custom_call" | custom-call | flops 1000000 | bytes 4194304 | tf_op jit(solution)/shard_map/unpack/pallas_call | solution.py:414
  (113 shorter events, 43.6 us)
Async XLA Ops:
  4.2 9.0 %collective-permute-start = (bf16[3,144,512]{2,1,0:T(8,128)(2,1)S(1)}, bf16[3,144,512]{2,1,0:T(8,128)(2,1)S(1)}, u32[]{:S(2)}, u32[]{:S(2)}) collective-permute-start(bf16[3,144,512]{2,1,0:T(8,128)(2,1)S(1)} %get-tuple-element.51), channel_id=1, source_target_pairs={{0,7},{1,2},{2,1},{3,4},{4,3},{5,6},{6,5},{7,0},{8,15},{9,10},{10,... | collective-permute-start | bytes 1327112 | tf_op jit(solution)/shard_map/ppermute | solution.py:273
  6.9 6.3 %collective-permute-start.1 = (bf16[3,144,512]{2,1,0:T(8,128)(2,1)S(1)}, bf16[3,144,512]{2,1,0:T(8,128)(2,1)S(1)}, u32[]{:S(2)}, u32[]{:S(2)}) collective-permute-start(bf16[3,144,512]{2,1,0:T(8,128)(2,1)S(1)} %get-tuple-element.53), channel_id=1, source_target_pairs={{0,1},{1,0},{2,3},{3,2},{4,5},{5,4},{6,7},{7,6},{8,9},{9,8},{10,11... | collective-permute-start | bytes 1327112 | tf_op jit(solution)/shard_map/ppermute | solution.py:273
  14.1 13.3 %collective-permute-start.3 = (bf16[3,144,512]{2,1,0:T(8,128)(2,1)S(1)}, bf16[3,144,512]{2,1,0:T(8,128)(2,1)S(1)}, u32[]{:S(2)}, u32[]{:S(2)}) collective-permute-start(bf16[3,144,512]{2,1,0:T(8,128)(2,1)S(1)} %pad_maximum_fusion.2), channel_id=1, source_target_pairs={{0,8},{1,9},{2,10},{3,11},{4,12},{5,13},{6,14},{7,15},{8,0},{9,1},... | collective-permute-start | bytes 1327112 | tf_op jit(solution)/shard_map/ppermute | solution.py:273
  39.0 5.7 %collective-permute-start.6 = (bf16[3,64,512]{2,1,0:T(8,128)(2,1)S(1)}, bf16[3,64,512]{2,1,0:T(8,128)(2,1)S(1)}, u32[]{:S(2)}, u32[]{:S(2)}) collective-permute-start(bf16[3,64,512]{2,1,0:T(8,128)(2,1)S(1)} %pad_maximum_fusion.9), channel_id=1, source_target_pairs={{0,7},{1,2},{2,1},{3,4},{4,3},{5,6},{6,5},{7,0},{8,15},{9,10},{10,... | collective-permute-start | bytes 589832 | tf_op jit(solution)/shard_map/ppermute | solution.py:273
  59.5 11.2 %collective-permute-start.11 = (bf16[64,512]{1,0:T(8,128)(2,1)S(1)}, bf16[64,512]{1,0:T(8,128)(2,1)S(1)}, u32[]{:S(2)}, u32[]{:S(2)}) collective-permute-start(bf16[64,512]{1,0:T(8,128)(2,1)S(1)} %get-tuple-element.105), channel_id=1, source_target_pairs={{0,8},{1,9},{2,10},{3,11},{4,12},{5,13},{6,14},{7,15},{8,0},{9,1},... | collective-permute-start | bytes 196616 | tf_op jit(solution)/shard_map/ppermute | solution.py:273
  64.7 6.0 %collective-permute-start.10 = (bf16[64,512]{1,0:T(8,128)(2,1)S(1)}, bf16[64,512]{1,0:T(8,128)(2,1)S(1)}, u32[]{:S(2)}, u32[]{:S(2)}) collective-permute-start(bf16[64,512]{1,0:T(8,128)(2,1)S(1)} %get-tuple-element.107), channel_id=1, source_target_pairs={{8,16},{9,17},{10,18},{11,19},{12,20},{13,21},{14,22},{15,23},{16,... | collective-permute-start | bytes 196616 | tf_op jit(solution)/shard_map/ppermute | solution.py:273
  67.8 8.8 %collective-permute-start.13 = (bf16[4,4,3,16,512]{4,3,2,1,0:T(8,128)(2,1)S(1)}, bf16[4,4,3,16,512]{4,3,2,1,0:T(8,128)(2,1)S(1)}, u32[]{:S(2)}, u32[]{:S(2)}) collective-permute-start(bf16[4,4,3,16,512]{4,3,2,1,0:T(8,128)(2,1)S(1)} %get-tuple-element.73), channel_id=1, source_target_pairs={{0,1},{1,0},{2,3},{3,2},{4,5},{5,4},{6,7},{7,6},{8,9},{9,8},{10,11... | collective-permute-start | bytes 2359304 | tf_op jit(solution)/shard_map/ppermute | solution.py:273
  79.3 13.4 %collective-permute-start.15 = (bf16[4,6,16,512]{3,2,1,0:T(8,128)(2,1)S(1)}, bf16[4,6,16,512]{3,2,1,0:T(8,128)(2,1)S(1)}, u32[]{:S(2)}, u32[]{:S(2)}) collective-permute-start(bf16[4,6,16,512]{3,2,1,0:T(8,128)(2,1)S(1)} %pad_maximum_fusion.4), channel_id=1, source_target_pairs={{0,4},{1,65},{2,6},{3,67},{4,0},{5,69},{6,2},{7,71},{8,12},{9,73},... | collective-permute-start | bytes 1179656 | tf_op jit(solution)/shard_map/ppermute | solution.py:273
  87.5 10.0 %collective-permute-start.16 = (bf16[4,6,16,512]{3,2,1,0:T(8,128)(2,1)S(1)}, bf16[4,6,16,512]{3,2,1,0:T(8,128)(2,1)S(1)}, u32[]{:S(2)}, u32[]{:S(2)}) collective-permute-start(bf16[4,6,16,512]{3,2,1,0:T(8,128)(2,1)S(1)} %pad_maximum_fusion.5), channel_id=1, source_target_pairs={{0,6},{1,97},{2,0},{3,99},{4,2},{5,101},{6,4},{7,103},{8,14},{9,10... | collective-permute-start | bytes 1179656 | tf_op jit(solution)/shard_map/ppermute | solution.py:273
  88.5 9.0 %collective-permute-start.14 = (bf16[4,6,16,512]{3,2,1,0:T(8,128)(2,1)S(1)}, bf16[4,6,16,512]{3,2,1,0:T(8,128)(2,1)S(1)}, u32[]{:S(2)}, u32[]{:S(2)}) collective-permute-start(bf16[4,6,16,512]{3,2,1,0:T(8,128)(2,1)S(1)} %pad_maximum_fusion.3), channel_id=1, source_target_pairs={{0,2},{1,33},{2,4},{3,35},{4,6},{5,37},{6,0},{7,39},{8,10},{9,41},... | collective-permute-start | bytes 1179656 | tf_op jit(solution)/shard_map/ppermute | solution.py:273
  89.1 8.6 %collective-permute-start.17 = (bf16[3,128,512]{2,1,0:T(8,128)(2,1)S(1)}, bf16[3,128,512]{2,1,0:T(8,128)(2,1)S(1)}, u32[]{:S(2)}, u32[]{:S(2)}) collective-permute-start(bf16[3,128,512]{2,1,0:T(8,128)(2,1)S(1)} %get-tuple-element.74), channel_id=1, source_target_pairs={{0,7},{1,2},{2,1},{3,4},{4,3},{5,6},{6,5},{7,0},{8,15},{9,10},{10,... | collective-permute-start | bytes 1179656 | tf_op jit(solution)/shard_map/ppermute | solution.py:273
  89.1 8.6 %collective-permute-start.18 = (bf16[3,128,512]{2,1,0:T(8,128)(2,1)S(1)}, bf16[3,128,512]{2,1,0:T(8,128)(2,1)S(1)}, u32[]{:S(2)}, u32[]{:S(2)}) collective-permute-start(bf16[3,128,512]{2,1,0:T(8,128)(2,1)S(1)} %get-tuple-element.75), channel_id=1, source_target_pairs={{0,1},{1,0},{2,3},{3,2},{4,5},{5,4},{6,7},{7,6},{8,9},{9,8},{10,11... | collective-permute-start | bytes 1179656 | tf_op jit(solution)/shard_map/ppermute | solution.py:273
  97.9 13.2 %collective-permute-start.22 = (bf16[3,128,512]{2,1,0:T(8,128)(2,1)S(1)}, bf16[3,128,512]{2,1,0:T(8,128)(2,1)S(1)}, u32[]{:S(2)}, u32[]{:S(2)}) collective-permute-start(bf16[3,128,512]{2,1,0:T(8,128)(2,1)S(1)} %pad_maximum_fusion.6), channel_id=1, source_target_pairs={{8,16},{9,17},{10,18},{11,19},{12,20},{13,21},{14,22},{15,23},{16,... | collective-permute-start | bytes 1179656 | tf_op jit(solution)/shard_map/ppermute | solution.py:273
  98.6 13.1 %collective-permute-start.23 = (bf16[3,128,512]{2,1,0:T(8,128)(2,1)S(1)}, bf16[3,128,512]{2,1,0:T(8,128)(2,1)S(1)}, u32[]{:S(2)}, u32[]{:S(2)}) collective-permute-start(bf16[3,128,512]{2,1,0:T(8,128)(2,1)S(1)} %pad_maximum_fusion.7), channel_id=1, source_target_pairs={{0,8},{1,9},{2,10},{3,11},{4,12},{5,13},{6,14},{7,15},{8,0},{9,1},... | collective-permute-start | bytes 1179656 | tf_op jit(solution)/shard_map/ppermute | solution.py:273
  104.2 6.1 %collective-permute-start.20 = (bf16[6,16,512]{2,1,0:T(8,128)(2,1)S(1)}, bf16[6,16,512]{2,1,0:T(8,128)(2,1)S(1)}, u32[]{:S(2)}, u32[]{:S(2)}) collective-permute-start(bf16[6,16,512]{2,1,0:T(8,128)(2,1)S(1)} %get-tuple-element.78), channel_id=1, source_target_pairs={{0,64},{1,5},{2,66},{3,7},{4,68},{5,1},{6,70},{7,3},{8,72},{9,13},... | collective-permute-start | bytes 294920 | tf_op jit(solution)/shard_map/ppermute | solution.py:273
  111.7 6.5 %collective-permute-start.26 = (bf16[6,16,512]{2,1,0:T(8,128)(2,1)S(1)}, bf16[6,16,512]{2,1,0:T(8,128)(2,1)S(1)}, u32[]{:S(2)}, u32[]{:S(2)}) collective-permute-start(bf16[6,16,512]{2,1,0:T(8,128)(2,1)S(1)} %add_convert_fusion.9), channel_id=1, source_target_pairs={{0,24},{1,25},{2,26},{3,27},{4,28},{5,29},{6,30},{7,31},{8,0},{9,1... | collective-permute-start | bytes 294920 | tf_op jit(solution)/shard_map/ppermute | solution.py:273
  116.6 5.7 %collective-permute-start.25 = (bf16[6,16,512]{2,1,0:T(8,128)(2,1)S(1)}, bf16[6,16,512]{2,1,0:T(8,128)(2,1)S(1)}, u32[]{:S(2)}, u32[]{:S(2)}) collective-permute-start(bf16[6,16,512]{2,1,0:T(8,128)(2,1)S(1)} %add_convert_fusion.9), channel_id=1, source_target_pairs={{0,8},{1,9},{2,10},{3,11},{4,12},{5,13},{6,14},{7,15},{8,16},{9,17... | collective-permute-start | bytes 294920 | tf_op jit(solution)/shard_map/ppermute | solution.py:273
  116.6 5.7 %collective-permute-start.24 = (bf16[6,16,512]{2,1,0:T(8,128)(2,1)S(1)}, bf16[6,16,512]{2,1,0:T(8,128)(2,1)S(1)}, u32[]{:S(2)}, u32[]{:S(2)}) collective-permute-start(bf16[6,16,512]{2,1,0:T(8,128)(2,1)S(1)} %add_convert_fusion.9), channel_id=1, source_target_pairs={{0,16},{1,17},{2,18},{3,19},{4,20},{5,21},{6,22},{7,23},{8,24},{9,... | collective-permute-start | bytes 294920 | tf_op jit(solution)/shard_map/ppermute | solution.py:273
  122.4 6.3 %collective-permute-start.29 = (bf16[6,16,512]{2,1,0:T(8,128)(2,1)S(1)}, bf16[6,16,512]{2,1,0:T(8,128)(2,1)S(1)}, u32[]{:S(2)}, u32[]{:S(2)}) collective-permute-start(bf16[6,16,512]{2,1,0:T(8,128)(2,1)S(1)} %add_convert_fusion.8), channel_id=1, source_target_pairs={{0,96},{1,7},{2,98},{3,1},{4,100},{5,3},{6,102},{7,5},{8,104},{9,1... | collective-permute-start | bytes 294920 | tf_op jit(solution)/shard_map/ppermute | solution.py:273
  126.0 5.7 %collective-permute-start.27 = (bf16[6,16,512]{2,1,0:T(8,128)(2,1)S(1)}, bf16[6,16,512]{2,1,0:T(8,128)(2,1)S(1)}, u32[]{:S(2)}, u32[]{:S(2)}) collective-permute-start(bf16[6,16,512]{2,1,0:T(8,128)(2,1)S(1)} %add_convert_fusion.8), channel_id=1, source_target_pairs={{0,32},{1,3},{2,34},{3,5},{4,36},{5,7},{6,38},{7,1},{8,40},{9,11},... | collective-permute-start | bytes 294920 | tf_op jit(solution)/shard_map/ppermute | solution.py:273
  131.9 9.3 %collective-permute-start.31 = (bf16[4,6,16,512]{3,2,1,0:T(8,128)(2,1)S(1)}, bf16[4,6,16,512]{3,2,1,0:T(8,128)(2,1)S(1)}, u32[]{:S(2)}, u32[]{:S(2)}) collective-permute-start(bf16[4,6,16,512]{3,2,1,0:T(8,128)(2,1)S(1)} %get-tuple-element.115), channel_id=1, source_target_pairs={{0,4},{1,65},{2,6},{3,67},{4,0},{5,69},{6,2},{7,71},{8,12},{9,73},... | collective-permute-start | bytes 1179656 | tf_op jit(solution)/shard_map/ppermute | solution.py:273
  134.7 10.8 %collective-permute-start.30 = (bf16[4,6,16,512]{3,2,1,0:T(8,128)(2,1)S(1)}, bf16[4,6,16,512]{3,2,1,0:T(8,128)(2,1)S(1)}, u32[]{:S(2)}, u32[]{:S(2)}) collective-permute-start(bf16[4,6,16,512]{3,2,1,0:T(8,128)(2,1)S(1)} %get-tuple-element.115), channel_id=1, source_target_pairs={{0,2},{1,33},{2,4},{3,35},{4,6},{5,37},{6,0},{7,39},{8,10},{9,41},... | collective-permute-start | bytes 1179656 | tf_op jit(solution)/shard_map/ppermute | solution.py:273
  135.1 10.4 %collective-permute-start.32 = (bf16[4,6,16,512]{3,2,1,0:T(8,128)(2,1)S(1)}, bf16[4,6,16,512]{3,2,1,0:T(8,128)(2,1)S(1)}, u32[]{:S(2)}, u32[]{:S(2)}) collective-permute-start(bf16[4,6,16,512]{3,2,1,0:T(8,128)(2,1)S(1)} %get-tuple-element.115), channel_id=1, source_target_pairs={{0,6},{1,97},{2,0},{3,99},{4,2},{5,101},{6,4},{7,103},{8,14},{9,10... | collective-permute-start | bytes 1179656 | tf_op jit(solution)/shard_map/ppermute | solution.py:273
  145.7 12.4 %collective-permute-start.33 = (bf16[4,4,6,16,512]{4,3,2,1,0:T(8,128)(2,1)S(1)}, bf16[4,4,6,16,512]{4,3,2,1,0:T(8,128)(2,1)S(1)}, u32[]{:S(2)}, u32[]{:S(2)}) collective-permute-start(bf16[4,4,6,16,512]{4,3,2,1,0:T(8,128)(2,1)S(1)} %pad_maximum_fusion.mine), channel_id=1, source_target_pairs={{0,1},{1,0},{2,3},{3,2},{4,5},{5,4},{6,7},{7,6},{8,9},{9,8},{10,11... | collective-permute-start | bytes 4718600 | tf_op jit(solution)/shard_map/ppermute | solution.py:273
  (24 other events, 253.7 us)
